TPU v7x, 512 devices: a whole 4x8x8 slice. The times are simulated.
512 devices in a mesh: attn: 64 (over z, y), ffn: 8 (over x, core).
Axes of the slice: x: 4, y: 8, z: 8, core: 2. Of those that a mesh axis runs over, the one named last changes fastest.
Arguments:
- residual: bfloat16 [512, 8192], P('attn', 'ffn'), may hold values from -12 to 12
- queries: bfloat16 [512, 8192], P('attn', 'ffn'), may hold values from -100 to 100
- cache_keys: bfloat16 [512, 8, 512, 128], P('attn', 'ffn'), may hold values from -4 to 4
- cache_values: bfloat16 [512, 8, 512, 128], P('attn', 'ffn'), may hold values from -6 to 6
- new_keys: bfloat16 [512, 8, 128], P('attn', 'ffn'), may hold values from -6 to 6
- new_values: bfloat16 [512, 8, 128], P('attn', 'ffn'), may hold values from -6 to 6
- lengths: int32 [512], P('attn'), may hold values from 1 to 512, as said below
- counts: int32 [64], P('attn'), may hold values from 1 to 8, 384 in all
- norm_gain: bfloat16 [8192], replicated, may hold values from 0.099609375 to 1.8984375
- gate_weight: bfloat16 [28672, 8192], P('attn', 'ffn'), may hold values from -0.0625 to 0.0625
- up_weight: bfloat16 [28672, 8192], P('attn', 'ffn'), may hold values from -0.0625 to 0.0625
- down_weight: bfloat16 [28672, 8192], P('attn', 'ffn'), may hold values from -0.09375 to 0.09375
Outputs:
- layer_out: bfloat16 [512, 8192], P('attn', 'ffn')
Inputs may be any that keep to these rules, and one draw needn't show every extreme that they name: `lengths`: one slot holds exactly 512 cached positions. The counts sum to 384; some attention index has all 8 slots live.
All inputs are finite; a program needn't handle non-finite values. No bound on the sum of `counts` on one device may be relied on, other than what follows from the above.
Results may differ from a plain program's by a relative error of at most 0.017.
Values may be sent and summed in bfloat16 or wider, within the bound.
A program may use at most 64 MiB of HBM per device.

v0:
```python
import jax
import jax.numpy as jnp
from jax import lax
from jax.sharding import PartitionSpec as P

D = 8192


epsilon = 1e-05


def attend(queries, cache_keys, cache_values, new_keys, new_values, lengths):
    slot_count = queries.shape[0]
    kv_dev = cache_keys.shape[1]
    ctx_len = cache_keys.shape[2]
    head_dim = cache_keys.shape[3]
    head_group = queries.shape[1] // (kv_dev * head_dim)
    score_scale = 1.0 / head_dim**0.5
    query_heads = queries.reshape(slot_count, kv_dev, head_group, head_dim)
    scores = (
        jnp.einsum("rgqd,rgpd->rgqp", query_heads, cache_keys, preferred_element_type=jnp.float32)
        * score_scale
    )
    positions = jnp.arange(ctx_len, dtype=jnp.int32)
    allowed = positions[None, None, None, :] < lengths[:, None, None, None]
    scores = jnp.where(allowed, scores, -1e30)
    own_score = (
        jnp.einsum("rgqd,rgd->rgq", query_heads, new_keys, preferred_element_type=jnp.float32)
        * score_scale
    )
    row_max = jnp.maximum(jnp.max(scores, axis=-1), own_score)
    key_weights = jnp.exp(scores - row_max[..., None])
    own_weight = jnp.exp(own_score - row_max)
    denominator = jnp.sum(key_weights, axis=-1) + own_weight
    key_probs = (key_weights / denominator[..., None]).astype(jnp.bfloat16)
    own_prob = (own_weight / denominator).astype(jnp.bfloat16)
    mixed = jnp.einsum(
        "rgqp,rgpd->rgqd", key_probs, cache_values, preferred_element_type=jnp.float32
    )
    mixed = (
        mixed
        + own_prob.astype(jnp.float32)[..., None] * new_values.astype(jnp.float32)[:, :, None, :]
    )
    return mixed.reshape(slot_count, kv_dev * head_group * head_dim).astype(jnp.bfloat16)


def activate(summed, units_dev):
    return (jax.nn.silu(summed[:, :units_dev]) * summed[:, units_dev:]).astype(jnp.bfloat16)


def on_device(
    residual,
    queries,
    cache_keys,
    cache_values,
    new_keys,
    new_values,
    lengths,
    counts,
    norm_gain,
    gate_weight,
    up_weight,
    down_weight,
):
    slot_count = residual.shape[0]
    width_dev = residual.shape[1]
    units_dev = gate_weight.shape[0]
    attention = attend(queries, cache_keys, cache_values, new_keys, new_values, lengths)
    attention = lax.optimization_barrier(attention)
    hidden = (residual.astype(jnp.float32) + attention.astype(jnp.float32)).astype(jnp.bfloat16)
    hidden_f32 = hidden.astype(jnp.float32)
    square_part = jnp.sum(hidden_f32 * hidden_f32, axis=-1)
    square_total = lax.psum(square_part, "ffn")
    mean_square = (square_total / D)[:, None]
    gain_block = lax.dynamic_slice_in_dim(norm_gain, lax.axis_index("ffn") * width_dev, width_dev)
    outgoing = (
        hidden_f32 * lax.rsqrt(mean_square + epsilon) * gain_block.astype(jnp.float32)
    ).astype(jnp.bfloat16)
    block_rows = lax.all_gather(outgoing, "attn", axis=0, tiled=True)
    gate_part = lax.dot_general(
        block_rows, gate_weight, (((1,), (1,)), ((), ())), preferred_element_type=jnp.float32
    )
    up_part = lax.dot_general(
        block_rows, up_weight, (((1,), (1,)), ((), ())), preferred_element_type=jnp.float32
    )
    paired = jnp.concatenate([gate_part, up_part], axis=1)
    summed = lax.psum(paired, "ffn")
    activated = activate(summed, units_dev)
    ffn_out = lax.psum_scatter(
        jnp.dot(activated, down_weight, preferred_element_type=jnp.float32),
        "attn",
        scatter_dimension=0,
        tiled=True,
    )
    slot_index = jnp.arange(slot_count, dtype=jnp.int32)
    is_live = slot_index < counts[0]
    result = jnp.where(is_live[:, None], hidden_f32 + ffn_out, 0.0)
    return result.astype(jnp.bfloat16)


def solution(mesh):
    return jax.shard_map(
        on_device,
        mesh=mesh,
        in_specs=(
            P("attn", "ffn"),
            P("attn", "ffn"),
            P("attn", "ffn", None, None),
            P("attn", "ffn", None, None),
            P("attn", "ffn", None),
            P("attn", "ffn", None),
            P("attn"),
            P("attn"),
            P(),
            P("attn", "ffn"),
            P("attn", "ffn"),
            P("attn", "ffn"),
        ),
        out_specs=P("attn", "ffn"),
        check_vma=False,
    )
```

profile of v0, /device:TPU:1, one launch (start us, length us, event | category | flops | bytes accessed | tf_op | source)
XLA Modules:
  0.0 361.0 jit_solution(4467214854007779511)
XLA Ops:
  6.5 0.0 copy-start
  6.5 0.0 all-gather.2.cloned.1.call-start
  6.5 0.9 iota_compare_fusion
  7.4 0.8 fusion.17
  8.3 0.0 copy-done
  8.3 1.2 fusion.24
  9.4 0.2 fusion.9
  9.6 0.7 bitcast_convert_fusion
  10.3 1.5 fusion.2
  11.9 0.0 copy-done.1
  11.9 0.1 fusion.12
  12.0 18.8 %psum.14 = f32[8]{0:T(128)S(1)} all-reduce(f32[8]{0:T(128)S(1)} %fusion.12), channel_id=1, replica_groups=mesh['attn'=64,'ffn'=8] {'ffn'}, use_global_device_ids=true, to_apply=%region_3.4 | all-reduce | flops 8 | bytes 64 | tf_op jit(solution)/shard_map/psum | solution.py:73
  30.8 0.7 dynamic-slice_convert_fusion
  31.5 0.7 fusion.14
  32.2 0.0 all-gather.2.cloned.1.call-update
  32.2 0.0 all-reduce.4.cloned.1.call-start
  32.2 76.6 %all-gather.2.cloned.1.call-done = bf16[512,1024]{1,0:T(8,128)(2,1)} async-done(((bf16[8,1024]{1,0:T(8,128)(2,1)}), bf16[512,1024]{1,0:T(8,128)(2,1)}) %all-gather.2.cloned.1.call-update) | async-done | bytes 1048592 | tf_op jit(solution)/shard_map/all_gather | solution.py:79
  108.9 0.0 copy-done.3
  108.9 2.0 fusion.25
  110.9 0.0 copy-done.4
  110.9 0.0 copy-done.2
  110.9 0.7 fusion.26
  111.6 1.4 pad_maximum_fusion
  113.0 0.0 all-reduce.4.cloned.1.call-update
  113.1 0.0 all-reduce.6.cloned.1.call-start
  113.1 75.3 %all-reduce.4.cloned.1.call-done = f32[512,896]{0,1:T(8,128)} async-done(((f32[512,896]{0,1:T(8,128)}), f32[512,896]{0,1:T(8,128)}) %all-reduce.4.cloned.1.call-update) | async-done | bytes 1835024 | tf_op jit(solution)/shard_map/psum | solution.py:87
  188.4 0.0 copy-done.5
  188.4 3.6 fusion.6
  192.0 0.0 all-reduce.6.cloned.1.call-update
  192.7 1.3 dynamic-slice
  194.7 158.4 %all-reduce.6.cloned.1.call-done = f32[512,1024]{1,0:T(8,128)} async-done(((f32[512,1024]{1,0:T(8,128)}), f32[512,1024]{1,0:T(8,128)}) %all-reduce.6.cloned.1.call-update) | async-done | bytes 2097168
  353.0 1.4 fusion.16
  (10 shorter events, 0.1 us)
Async XLA Ops:
  6.5 1.7 copy-start
  6.5 5.3 %copy-start.1 = (bf16[8,1024]{1,0:T(8,128)(2,1)S(1)}, bf16[8,1024]{1,0:T(8,128)(2,1)}, u32[]{:S(2)}) copy-start(bf16[8,1024]{1,0:T(8,128)(2,1)} %param.12) | copy-start | bytes 49156
  6.5 102.3 %copy-start.3 = (bf16[448,1024]{1,0:T(8,128)(2,1)S(1)}, bf16[448,1024]{1,0:T(8,128)(2,1)}, u32[]{:S(2)}) copy-start(bf16[448,1024]{1,0:T(8,128)(2,1)} %param.21) | copy-start | bytes 2752516
  6.5 102.3 %all-gather.2.cloned.1.call-start = ((), (), s32[]{:S(2)}) async-start(), calls=%async_computation | async-start | bytes 1064960 | tf_op jit(solution)/shard_map/all_gather | solution.py:79
  11.9 99.0 %copy-start.4 = (bf16[448,1024]{1,0:T(8,128)(2,1)S(1)}, bf16[448,1024]{1,0:T(8,128)(2,1)}, u32[]{:S(2)}) copy-start(bf16[448,1024]{1,0:T(8,128)(2,1)} %param.22) | copy-start | bytes 2752516
  32.2 156.2 %all-reduce.4.cloned.1.call-start = ((), (), s32[]{:S(2)}) async-start(), calls=%async_computation.1 | async-start | bytes 3670016 | tf_op jit(solution)/shard_map/psum | solution.py:87
  108.9 2.1 copy-start.2
  113.0 75.4 %copy-start.5 = (bf16[448,1024]{1,0:T(8,128)(2,1)S(1)}, bf16[448,1024]{1,0:T(8,128)(2,1)}, u32[]{:S(2)}) copy-start(bf16[448,1024]{1,0:T(8,128)(2,1)} %param.23) | copy-start | bytes 2752516
  113.1 240.0 %all-reduce.6.cloned.1.call-start = ((), (), s32[]{:S(2)}) async-start(), calls=%async_computation.2 | async-start | bytes 4194304
Sparse Core Ops, SparseCore 0:
  32.3 76.4 all-gather.1
  113.2 75.2 all-reduce.3
  192.2 160.8 all-reduce.5
where the time goes:
time: 364 us; the launch traced here: 361 us
  waiting for transfers between devices  310 us (85%)
  blocking collectives  18.8 us (5%)
  between operations  14.5 us (4%)
  matrix products  9.87 us (3%)
  other arithmetic  6.1 us (2%)
    unnamed x4, waiting for transfers between devices  158 us
    all_gather x1, waiting for transfers between devices, on_device(): block_rows = lax.all_gather(outgoing, 'attn', axis=0, tiled=True)  76.6 us
    psum x1, waiting for transfers between devices, on_device(): summed = lax.psum(paired, 'ffn')  75.3 us
    psum x1, blocking collectives, on_device(): square_total = lax.psum(square_part, 'ffn')  18.8 us
  transfers between devices with their start and end apart: 3, of which 3 were waited for; matrix products, arithmetic and copies ran while one was open for 0% of the time, Pallas kernels for 0%

commit v1 on v0

--- a/solution.py
+++ b/solution.py
@@ -1,6 +1,8 @@
 import jax
 import jax.numpy as jnp
 from jax import lax
+from jax.experimental import pallas as pl
+from jax.experimental.pallas import tpu as pltpu
 from jax.sharding import PartitionSpec as P
 
 D = 8192
@@ -44,8 +46,282 @@
     return mixed.reshape(slot_count, kv_dev * head_group * head_dim).astype(jnp.bfloat16)
 
 
-def activate(summed, units_dev):
-    return (jax.nn.silu(summed[:, :units_dev]) * summed[:, units_dev:]).astype(jnp.bfloat16)
+MESH = pl.DeviceIdType.MESH
+N = 8
+NX = 4
+HALF = 512
+UNITS = 448
+MAIN = 384
+TILES = ((0, 256), (256, 256), (512, 256), (768, 128))
+
+
+def transposed_dot(rows, weight):
+    return lax.dot_general(rows, weight, (((1,), (1,)), ((), ())), preferred_element_type=jnp.float32)
+
+
+def kernel(
+    hidden_ref,
+    gain_ref,
+    gate_hbm,
+    up_hbm,
+    down_hbm,
+    out_ref,
+    gu,
+    down,
+    ga,
+    gb,
+    xs,
+    ssb,
+    pair_out,
+    pair_in,
+    pair_ss,
+    own,
+    x_out,
+    x_in,
+    x_ss_out,
+    x_ss_in,
+    act,
+    da,
+    db,
+    ra,
+    rb,
+    d2a,
+    d2b,
+    r2a,
+    r2b,
+    wsem,
+    g1s,
+    g1r,
+    g2s,
+    g2r,
+    ps,
+    pr,
+    xsd,
+    xrv,
+    acs,
+    acr,
+    r1s,
+    r1r,
+    r2s,
+    r2r,
+):
+    attn = lax.axis_index("attn")
+    ffn = lax.axis_index("ffn")
+    z, y = lax.div(attn, N), lax.rem(attn, N)
+    x, c = lax.div(ffn, 2), lax.rem(ffn, 2)
+
+    def at(zz, yy, xx, cc):
+        return (zz * N + yy, xx * 2 + cc)
+
+    def past(i, k, n):
+        return lax.rem(i + k, n)
+
+    loads = [
+        pltpu.make_async_copy(gate_hbm, gu.at[pl.ds(0, UNITS)], wsem.at[0]),
+        pltpu.make_async_copy(up_hbm.at[pl.ds(MAIN, UNITS - MAIN)], gu.at[pl.ds(UNITS, UNITS - MAIN)], wsem.at[1]),
+        pltpu.make_async_copy(up_hbm.at[pl.ds(0, MAIN)], gu.at[pl.ds(512, MAIN)], wsem.at[2]),
+        pltpu.make_async_copy(down_hbm, down, wsem.at[3]),
+    ]
+    for load in loads:
+        load.start()
+
+    barrier = pltpu.get_barrier_semaphore()
+    partners = [at(past(z, k, N), y, x, c) for k in range(1, N)]
+    partners += [at(z, past(y, k, N), x, c) for k in range(1, N)]
+    partners += [at(z, y, past(x, k // 2, NX), past(c, k % 2, 2)) for k in range(1, 2 * NX)]
+    for partner in partners:
+        pl.semaphore_signal(barrier, inc=1, device_id=partner, device_id_type=MESH)
+    pl.semaphore_wait(barrier, len(partners))
+
+    sent = []
+
+    def send(source, target, send_sem, recv_sem, device):
+        copy = pltpu.make_async_remote_copy(
+            src_ref=source, dst_ref=target, send_sem=send_sem, recv_sem=recv_sem, device_id=device, device_id_type=MESH
+        )
+        copy.start()
+        sent.append(copy)
+        return copy
+
+    ga[z, y] = hidden_ref[:, :HALF]
+    gb[y, z] = hidden_ref[:, HALF:]
+    first = []
+    for k in range(1, N):
+        first.append(send(ga.at[z, y], ga.at[z, y], g1s.at[0, k], g1r.at[0, k], at(z, past(y, k, N), x, c)))
+        first.append(send(gb.at[y, z], gb.at[y, z], g1s.at[1, k], g1r.at[1, k], at(past(z, k, N), y, x, c)))
+    for copy in first:
+        copy.wait_recv()
+    second = []
+    for k in range(1, N):
+        second.append(send(ga.at[z], ga.at[z], g2s.at[0, k], g2r.at[0, k], at(past(z, k, N), y, x, c)))
+        second.append(send(gb.at[y], gb.at[y], g2s.at[1, k], g2r.at[1, k], at(z, past(y, k, N), x, c)))
+    for copy in second:
+        copy.wait_recv()
+
+    gain_a = gain_ref[:, :HALF]
+    gain_b = gain_ref[:, HALF:]
+    lane = lax.broadcasted_iota(jnp.int32, (64, 128), 1)
+    row = lax.broadcasted_iota(jnp.int32, (64, 128), 0)
+    diagonal = lane == row
+
+    def scale(zz, carry):
+        place = lax.rem(zz, 2) * 4 + lax.div(zz, 2)
+        part_a = ga[zz].astype(jnp.float32).reshape(64, HALF)
+        part_b = gb[:, zz].astype(jnp.float32).reshape(64, HALF)
+        squares = jnp.sum(part_a * part_a + part_b * part_b, axis=1, keepdims=True)
+        ssb[place] = jnp.sum(jnp.where(diagonal, squares, 0.0), axis=0, keepdims=True)
+        xs[place, :, :HALF] = (part_a * gain_a).astype(jnp.bfloat16)
+        xs[place, :, HALF:] = (part_b * gain_b).astype(jnp.bfloat16)
+        return carry
+
+    lax.fori_loop(0, N, scale, 0)
+    for load in loads:
+        load.wait()
+
+    rows = xs[pl.ds((1 - c) * 4, 4)].reshape(256, 1024)
+    for start, width in TILES:
+        block = transposed_dot(rows, gu[start : start + width, :])
+        pair_out[:, :, start : start + width] = block.astype(jnp.bfloat16).reshape(4, 64, width)
+    other = at(z, y, x, 1 - c)
+    pair = [
+        send(pair_out, pair_in, ps.at[0], pr.at[0], other),
+        send(ssb.at[pl.ds((1 - c) * 4, 4)], pair_ss, ps.at[1], pr.at[1], other),
+    ]
+    rows = xs[pl.ds(c * 4, 4)].reshape(256, 1024)
+    for start, width in TILES:
+        own[:, :, start : start + width] = transposed_dot(rows, gu[start : start + width, :]).reshape(4, 64, width)
+    for copy in pair:
+        copy.wait_recv()
+    across = []
+    for k in range(1, NX):
+        xx = past(x, k, NX)
+        x_out[k] = (own[xx] + pair_in[xx].astype(jnp.float32)).astype(jnp.bfloat16)
+        x_ss_out[k] = ssb[c * 4 + xx] + pair_ss[xx]
+        across.append(send(x_out.at[k], x_in.at[k], xsd.at[0, k], xrv.at[0, k], at(z, y, xx, c)))
+        across.append(send(x_ss_out.at[k], x_ss_in.at[k], xsd.at[1, k], xrv.at[1, k], at(z, y, xx, c)))
+    total = own[x] + pair_in[x].astype(jnp.float32)
+    squares = ssb[c * 4 + x] + pair_ss[x]
+    for copy in across:
+        copy.wait_recv()
+    for k in range(1, NX):
+        total = total + x_in[k].astype(jnp.float32)
+        squares = squares + x_ss_in[k]
+    mean_square = jnp.sum(jnp.where(diagonal, squares, 0.0), axis=1, keepdims=True) / D
+    total = total * lax.rsqrt(mean_square + epsilon)
+    gate = total[:, :512]
+    silu = gate / (1.0 + jnp.exp(-gate))
+    act[ffn, :, :MAIN] = (silu[:, :MAIN] * total[:, 512:]).astype(jnp.bfloat16)
+    tail = silu[:, MAIN:] * pltpu.roll(total[:, MAIN:512], 64, 1)
+    act[ffn, :, MAIN:] = tail[:, : UNITS - MAIN].astype(jnp.bfloat16)
+    spread = []
+    for k in range(1, 2 * NX):
+        device = at(z, y, past(x, k // 2, NX), past(c, k % 2, 2))
+        spread.append(send(act.at[ffn], act.at[ffn], acs.at[k], acr.at[k], device))
+    for copy in spread:
+        copy.wait_recv()
+
+    ones = []
+    for half, (buffer, back) in enumerate(((da, ra), (db, rb))):
+        for m in range(2):
+            rows = act[4 * m : 4 * m + 4].reshape(256, UNITS)
+            for start in (0, 256):
+                block = jnp.dot(
+                    rows, down[:, half * HALF + start : half * HALF + start + 256], preferred_element_type=jnp.float32
+                ).astype(jnp.bfloat16)
+                block = block.reshape(4, N, 8, 256)
+                if half == 0:
+                    buffer[4 * m : 4 * m + 4, :, :, start : start + 256] = block
+                else:
+                    for i in range(4):
+                        buffer[:, 4 * m + i, :, start : start + 256] = block[i]
+        for k in range(1, N):
+            if half == 0:
+                there, device = past(z, k, N), at(past(z, k, N), y, x, c)
+            else:
+                there, device = past(y, k, N), at(z, past(y, k, N), x, c)
+            ones.append(send(buffer.at[there], back.at[k], r1s.at[half, k], r1r.at[half, k], device))
+    twos = []
+    for half, (buffer, back, onward, last) in enumerate(((da, ra, d2a, r2a), (db, rb, d2b, r2b))):
+        here = z if half == 0 else y
+        for copy in ones[half * 7 : half * 7 + 7]:
+            copy.wait_recv()
+        added = buffer[here].astype(jnp.float32)
+        for k in range(1, N):
+            added = added + back[k].astype(jnp.float32)
+        onward[...] = added.astype(jnp.bfloat16)
+        for k in range(1, N):
+            if half == 0:
+                there, device = past(y, k, N), at(z, past(y, k, N), x, c)
+            else:
+                there, device = past(z, k, N), at(past(z, k, N), y, x, c)
+            twos.append(send(onward.at[there], last.at[k], r2s.at[half, k], r2r.at[half, k], device))
+    for half, (onward, last) in enumerate(((d2a, r2a), (d2b, r2b))):
+        here = y if half == 0 else z
+        for copy in twos[half * 7 : half * 7 + 7]:
+            copy.wait_recv()
+        added = onward[here].astype(jnp.float32)
+        for k in range(1, N):
+            added = added + last[k].astype(jnp.float32)
+        out_ref[:, half * HALF : half * HALF + HALF] = added
+    for copy in sent:
+        copy.wait_send()
+
+
+def feed_forward(hidden, gain, gate_weight, up_weight, down_weight):
+    bf, f32 = jnp.bfloat16, jnp.float32
+    dma = pltpu.SemaphoreType.DMA
+    vmem = pltpu.VMEM
+    return pl.pallas_call(
+        kernel,
+        out_shape=jax.ShapeDtypeStruct((8, 1024), f32),
+        in_specs=[pl.BlockSpec(memory_space=vmem)] * 2 + [pl.BlockSpec(memory_space=pl.ANY)] * 3,
+        out_specs=pl.BlockSpec(memory_space=vmem),
+        scratch_shapes=[
+            vmem((896, 1024), bf),
+            vmem((UNITS, 1024), bf),
+            vmem((N, N, 8, HALF), bf),
+            vmem((N, N, 8, HALF), bf),
+            vmem((N, 64, 1024), bf),
+            vmem((N, 1, 128), f32),
+            vmem((4, 64, 896), bf),
+            vmem((4, 64, 896), bf),
+            vmem((4, 1, 128), f32),
+            vmem((4, 64, 896), f32),
+            vmem((NX, 64, 896), bf),
+            vmem((NX, 64, 896), bf),
+            vmem((NX, 1, 128), f32),
+            vmem((NX, 1, 128), f32),
+            vmem((2 * NX, 64, UNITS), bf),
+            vmem((N, N, 8, HALF), bf),
+            vmem((N, N, 8, HALF), bf),
+            vmem((N, N, 8, HALF), bf),
+            vmem((N, N, 8, HALF), bf),
+            vmem((N, 8, HALF), bf),
+            vmem((N, 8, HALF), bf),
+            vmem((N, 8, HALF), bf),
+            vmem((N, 8, HALF), bf),
+            dma((4,)),
+            dma((2, N)),
+            dma((2, N)),
+            dma((2, N)),
+            dma((2, N)),
+            dma((2,)),
+            dma((2,)),
+            dma((2, NX)),
+            dma((2, NX)),
+            dma((2 * NX,)),
+            dma((2 * NX,)),
+            dma((2, N)),
+            dma((2, N)),
+            dma((2, N)),
+            dma((2, N)),
+        ],
+        compiler_params=pltpu.CompilerParams(
+            collective_id=0, has_side_effects=True, vmem_limit_bytes=40 * 1024 * 1024
+        ),
+        cost_estimate=pl.CostEstimate(flops=1_400_000_000, bytes_accessed=3_000_000, transcendentals=0),
+        name="feed_forward",
+    )(hidden, gain, gate_weight, up_weight, down_weight)
 
 
 def on_device(
@@ -64,37 +340,13 @@
 ):
     slot_count = residual.shape[0]
     width_dev = residual.shape[1]
-    units_dev = gate_weight.shape[0]
     attention = attend(queries, cache_keys, cache_values, new_keys, new_values, lengths)
-    attention = lax.optimization_barrier(attention)
     hidden = (residual.astype(jnp.float32) + attention.astype(jnp.float32)).astype(jnp.bfloat16)
-    hidden_f32 = hidden.astype(jnp.float32)
-    square_part = jnp.sum(hidden_f32 * hidden_f32, axis=-1)
-    square_total = lax.psum(square_part, "ffn")
-    mean_square = (square_total / D)[:, None]
     gain_block = lax.dynamic_slice_in_dim(norm_gain, lax.axis_index("ffn") * width_dev, width_dev)
-    outgoing = (
-        hidden_f32 * lax.rsqrt(mean_square + epsilon) * gain_block.astype(jnp.float32)
-    ).astype(jnp.bfloat16)
-    block_rows = lax.all_gather(outgoing, "attn", axis=0, tiled=True)
-    gate_part = lax.dot_general(
-        block_rows, gate_weight, (((1,), (1,)), ((), ())), preferred_element_type=jnp.float32
-    )
-    up_part = lax.dot_general(
-        block_rows, up_weight, (((1,), (1,)), ((), ())), preferred_element_type=jnp.float32
-    )
-    paired = jnp.concatenate([gate_part, up_part], axis=1)
-    summed = lax.psum(paired, "ffn")
-    activated = activate(summed, units_dev)
-    ffn_out = lax.psum_scatter(
-        jnp.dot(activated, down_weight, preferred_element_type=jnp.float32),
-        "attn",
-        scatter_dimension=0,
-        tiled=True,
-    )
-    slot_index = jnp.arange(slot_count, dtype=jnp.int32)
-    is_live = slot_index < counts[0]
-    result = jnp.where(is_live[:, None], hidden_f32 + ffn_out, 0.0)
+    gain = gain_block.astype(jnp.float32)[None, :]
+    ffn_out = feed_forward(hidden, gain, gate_weight, up_weight, down_weight)
+    is_live = jnp.arange(slot_count, dtype=jnp.int32) < counts[0]
+    result = jnp.where(is_live[:, None], hidden.astype(jnp.float32) + ffn_out, 0.0)
     return result.astype(jnp.bfloat16)
 
 

time: 364 us -> 83 us (0.23)
  waiting for transfers between devices: 310 us -> 0 us
  Pallas kernels: 0 us -> 75.1 us
  blocking collectives: 18.8 us -> 0 us
  between operations: 14.5 us -> 0.73 us
  matrix products: 9.87 us -> 2.9 us
  other arithmetic: 6.1 us -> 1.67 us
    unnamed x4 -> x0, waiting for transfers between devices: 158 us -> none
    all_gather x1 -> x0, waiting for transfers between devices: 76.6 us -> none  [on_device(): block_rows = lax.all_gather(outgoing, 'attn', axis=0, tiled=True)]
    psum x1 -> x0, waiting for transfers between devices: 75.3 us -> none  [on_device(): summed = lax.psum(paired, 'ffn')]
    pallas_call x0 -> x1, Pallas kernels: none -> 75.1 us  [feed_forward(): pl.pallas_call(kernel, out_shape=jax.ShapeDtypeStruct((8, 1024), f32), in...]
    psum x1 -> x0, blocking collectives: 18.8 us -> none  [on_device(): square_total = lax.psum(square_part, 'ffn')]
    dot_general x3 -> x0, matrix products: 6.34 us -> none  [the longest x1 3.59 us: on_device(): jnp.dot(activated, down_weight, preferred_element_type=jnp.float32)]
  transfers between devices with their start and end apart: 3 -> 0, of which waited for: 3 -> 0; matrix products, arithmetic and copies ran while one was open for 0% -> 0% of each run, Pallas kernels for 0% -> 0%
where the time goes in v1:
time: 83 us; the launch traced here: 82.8 us
  Pallas kernels  75.1 us (90%)
  matrix products  2.9 us (3%)
  local copies, waits for them, and re-layouts  2.37 us (3%)
  other arithmetic  1.67 us (2%)
    pallas_call x1, Pallas kernels, feed_forward(): pl.pallas_call(kernel, out_shape=jax.ShapeDtypeStruct((8, 1024), f32), in...  75.1 us
    unnamed x18, local copies, waits for them, and re-layouts  2.37 us

profile of v1, /device:TPU:1, one launch (start us, length us, event | category | flops | bytes accessed | tf_op | source)
XLA Modules:
  0.0 82.8 jit_solution(379021247614009894)
XLA Ops:
  0.0 0.0 copy-start
  0.0 0.0 copy-start.7
  0.0 0.7 copy-done.7
  0.7 0.1 iota_compare_fusion
  0.8 0.4 copy-done
  1.2 0.0 copy-start.4
  1.2 0.0 copy-start.8
  1.2 0.0 copy-start.6
  1.2 0.0 copy-start.2
  1.3 1.3 %fusion.16 = (f32[8,8]{1,0:T(8,128)S(1)}, f32[8,8,512]{2,1,0:T(8,128)S(1)}) fusion(bf16[8,1,512,128]{3,2,1,0:T(8,128)(2,1)S(1)} %copy-done, bf16[8,8,128]{2,0,1:T(8,128)(2,1)} %bitcast.26, pred[8,512]{1,0:T(8,128)(4,1)S(1)} %iota_compare_fusion), kind=kOutput, calls=%fused_computation.29 | convolution fusion | flops 8486848 | bytes 1200384 | tf_op jit(solution)/shard_map/rgqd,rgpd->rgqp/dot_general | solution.py:23
  2.5 0.0 copy-start.1
  2.5 0.0 copy-done.4
  2.5 0.0 copy-done.8
  2.5 0.1 fusion.10
  2.7 0.2 fusion.6
  2.9 0.0 copy-done.6
  2.9 0.0 copy-start.5
  2.9 1.5 %fusion.3 = f32[1,8,8,128]{3,2,1,0:T(8,128)S(1)} fusion(bf16[8,1,512,128]{3,2,1,0:T(8,128)(2,1)} %param.15, f32[8,8,512]{2,1,0:T(8,128)S(1)} %get-tuple-element.8, f32[8,8]{1,0:T(8,128)S(1)} %get-tuple-element.6, f32[8,8]{1,0:T(8,128)S(1)} %multiply_maximum_fusion, f32[8,128]{1,0:T(8,128)S(1)} %bitcast_convert_fusion, f32[8,8]{1,0:T(8,128)S(1)} %get-tuple-element.5), kind=kOutput, calls=%fused_computation.5 | convolution fusion | flops 8519680 | bytes 1217280 | tf_op jit(solution)/shard_map/rgqp,rgpd->rgqd/dot_general | solution.py:39
  4.4 0.0 copy-done.5
  4.4 0.7 dynamic-slice_convert_fusion
  5.1 0.0 copy-done.2
  5.1 0.0 copy-done.1
  5.1 0.0 copy-start.3
  5.1 1.2 %copy-done.3 = bf16[448,1024]{1,0:T(8,128)(2,1)S(1)} copy-done((bf16[448,1024]{1,0:T(8,128)(2,1)S(1)}, bf16[448,1024]{1,0:T(8,128)(2,1)}, u32[]{:S(2)}) %copy-start.3) | copy-done | bytes 917528
  6.3 75.1 %feed_forward.1 = f32[8,1024]{1,0:T(8,128)S(1)} custom-call(bf16[8,1024]{1,0:T(8,128)(2,1)S(1)} %fusion.9.hidden_ref, f32[1,1024]{1,0:T(1,128)S(1)} %bitcast.25, bf16[448,1024]{1,0:T(8,128)(2,1)S(1)} %copy-done.1, bf16[448,1024]{1,0:T(8,128)(2,1)S(1)} %copy-done.2, bf16[448,1024]{1,0:T(8,128)(2,1)S(1)} %copy-done.3), custom_call_target="tpu_custom_call" | custom-call | flops 1400000000 | bytes 3000000 | tf_op jit(solution)/shard_map/feed_forward/pallas_call | solution.py:274
  82.1 0.7 select_convert_fusion
  (5 shorter events, 0.0 us)
Async XLA Ops:
  0.0 1.2 %copy-start = (bf16[8,1,512,128]{3,2,1,0:T(8,128)(2,1)S(1)}, bf16[8,1,512,128]{3,2,1,0:T(8,128)(2,1)}, u32[]{:S(2)}) copy-start(bf16[8,1,512,128]{3,2,1,0:T(8,128)(2,1)} %param.14) | copy-start | bytes 3145732
  0.0 0.7 copy-start.7
  1.2 1.3 %copy-start.4 = (bf16[8,1024]{1,0:T(8,128)(2,1)S(1)}, bf16[8,1024]{1,0:T(8,128)(2,1)}, u32[]{:S(2)}) copy-start(bf16[8,1024]{1,0:T(8,128)(2,1)} %param.13) | copy-start | bytes 49156
  1.2 1.3 %copy-start.8 = (bf16[8,1,128]{2,0,1:T(8,128)(2,1)S(1)}, bf16[8,1,128]{2,0,1:T(8,128)(2,1)}, u32[]{:S(2)}) copy-start(bf16[8,1,128]{2,0,1:T(8,128)(2,1)} %param.16) | copy-start | bytes 6148
  1.2 1.6 %copy-start.6 = (bf16[8,1,128]{2,0,1:T(8,128)(2,1)S(1)}, bf16[8,1,128]{2,0,1:T(8,128)(2,1)}, u32[]{:S(2)}) copy-start(bf16[8,1,128]{2,0,1:T(8,128)(2,1)} %param.17) | copy-start | bytes 6148
  1.2 3.9 %copy-start.2 = (bf16[448,1024]{1,0:T(8,128)(2,1)S(1)}, bf16[448,1024]{1,0:T(8,128)(2,1)}, u32[]{:S(2)}) copy-start(bf16[448,1024]{1,0:T(8,128)(2,1)} %up_hbm.1) | copy-start | bytes 2752516
  2.5 2.6 %copy-start.1 = (bf16[448,1024]{1,0:T(8,128)(2,1)S(1)}, bf16[448,1024]{1,0:T(8,128)(2,1)}, u32[]{:S(2)}) copy-start(bf16[448,1024]{1,0:T(8,128)(2,1)} %gate_hbm.1) | copy-start | bytes 2752516
  2.9 1.5 %copy-start.5 = (bf16[8,1024]{1,0:T(8,128)(2,1)S(1)}, bf16[8,1024]{1,0:T(8,128)(2,1)}, u32[]{:S(2)}) copy-start(bf16[8,1024]{1,0:T(8,128)(2,1)} %param.12) | copy-start | bytes 49156
  5.1 1.2 %copy-start.3 = (bf16[448,1024]{1,0:T(8,128)(2,1)S(1)}, bf16[448,1024]{1,0:T(8,128)(2,1)}, u32[]{:S(2)}) copy-start(bf16[448,1024]{1,0:T(8,128)(2,1)} %down_hbm.1) | copy-start | bytes 2752516

commit v2 on v0

--- a/solution.py
+++ b/solution.py
@@ -1,6 +1,8 @@
 import jax
 import jax.numpy as jnp
 from jax import lax
+from jax.experimental import pallas as pl
+from jax.experimental.pallas import tpu as pltpu
 from jax.sharding import PartitionSpec as P
 
 D = 8192
@@ -44,8 +46,352 @@
     return mixed.reshape(slot_count, kv_dev * head_group * head_dim).astype(jnp.bfloat16)
 
 
-def activate(summed, units_dev):
-    return (jax.nn.silu(summed[:, :units_dev]) * summed[:, units_dev:]).astype(jnp.bfloat16)
+MESH = pl.DeviceIdType.MESH
+N = 8
+NX = 4
+PARTS = 2
+QUARTER = 256
+UNITS = 448
+MAIN = 384
+TILES = ((0, 256), (256, 256), (512, 256), (768, 128))
+
+
+def transposed_dot(rows, weight):
+    return lax.dot_general(rows, weight, (((1,), (1,)), ((), ())), preferred_element_type=jnp.float32)
+
+
+def exchange(low, high):
+    axis = low.ndim - 2
+    upper = lax.broadcasted_iota(jnp.int32, low.shape, axis) < 4
+    return jnp.where(upper, low, pltpu.roll(high, 4, axis)), jnp.where(upper, pltpu.roll(low, 4, axis), high)
+
+
+def kernel(
+    hidden_ref,
+    gain_ref,
+    gate_hbm,
+    up_hbm,
+    down_hbm,
+    out_ref,
+    gu,
+    down,
+    ga,
+    gb,
+    xs,
+    ssb,
+    pair_out,
+    pair_in,
+    pair_ss,
+    own,
+    x_out,
+    x_in,
+    x_ss_out,
+    x_ss_in,
+    act,
+    da,
+    db,
+    ra,
+    rb,
+    d2a,
+    d2b,
+    r2a,
+    r2b,
+    wsem,
+    g1s,
+    g1r,
+    g2s,
+    g2r,
+    ps,
+    pr,
+    xsd,
+    xrv,
+    acs,
+    acr,
+    fws,
+    fwr,
+    r1s,
+    r1r,
+    r2s,
+    r2r,
+):
+    attn = lax.axis_index("attn")
+    ffn = lax.axis_index("ffn")
+    z, y = lax.div(attn, N), lax.rem(attn, N)
+    x, c = lax.div(ffn, 2), lax.rem(ffn, 2)
+
+    def at(zz, yy, xx, cc):
+        return (zz * N + yy, xx * 2 + cc)
+
+    def past(i, k, n):
+        return lax.rem(i + k, n)
+
+    loads = [
+        pltpu.make_async_copy(gate_hbm, gu.at[pl.ds(0, UNITS)], wsem.at[0]),
+        pltpu.make_async_copy(up_hbm.at[pl.ds(MAIN, UNITS - MAIN)], gu.at[pl.ds(UNITS, UNITS - MAIN)], wsem.at[1]),
+        pltpu.make_async_copy(up_hbm.at[pl.ds(0, MAIN)], gu.at[pl.ds(512, MAIN)], wsem.at[2]),
+        pltpu.make_async_copy(down_hbm, down, wsem.at[3]),
+    ]
+    for load in loads:
+        load.start()
+
+    barrier = pltpu.get_barrier_semaphore()
+    partners = [at(past(z, k, N), y, x, c) for k in range(1, N)]
+    partners += [at(z, past(y, k, N), x, c) for k in range(1, N)]
+    partners += [at(z, y, past(x, k, NX), c) for k in range(1, NX)]
+    partners += [at(z, y, x, 1 - c)]
+    for partner in partners:
+        pl.semaphore_signal(barrier, inc=1, device_id=partner, device_id_type=MESH)
+    pl.semaphore_wait(barrier, len(partners))
+
+    sent = []
+
+    def send(source, target, send_sem, recv_sem, device):
+        copy = pltpu.make_async_remote_copy(
+            src_ref=source, dst_ref=target, send_sem=send_sem, recv_sem=recv_sem, device_id=device, device_id_type=MESH
+        )
+        copy.start()
+        sent.append(copy)
+        return copy
+
+    other = at(z, y, x, 1 - c)
+    lane = lax.broadcasted_iota(jnp.int32, (32, 128), 1)
+    row = lax.broadcasted_iota(jnp.int32, (32, 128), 0)
+    diagonal = lane == row
+
+    def along(first_is_z, k):
+        if first_is_z:
+            return past(z, k, N), at(past(z, k, N), y, x, c)
+        return past(y, k, N), at(z, past(y, k, N), x, c)
+
+    wide = hidden_ref[...].astype(jnp.float32)
+    for buffer, start, one, two in ((ga, 0, z, y), (gb, 512, y, z)):
+        blocks = exchange(wide[:, start : start + QUARTER], wide[:, start + QUARTER : start + 512])
+        for p in range(PARTS):
+            buffer[p, one, two] = blocks[p].astype(jnp.bfloat16)
+
+    def gather_first(p):
+        copies = []
+        for k in range(1, N):
+            copies.append(send(ga.at[p, z, y], ga.at[p, z, y], g1s.at[p, 0, k], g1r.at[p, 0, k], along(False, k)[1]))
+            copies.append(send(gb.at[p, y, z], gb.at[p, y, z], g1s.at[p, 1, k], g1r.at[p, 1, k], along(True, k)[1]))
+        return copies
+
+    def gather_second(p, before):
+        for copy in before:
+            copy.wait_recv()
+        copies = []
+        for k in range(1, N):
+            copies.append(send(ga.at[p, z], ga.at[p, z], g2s.at[p, 0, k], g2r.at[p, 0, k], along(True, k)[1]))
+            copies.append(send(gb.at[p, y], gb.at[p, y], g2s.at[p, 1, k], g2r.at[p, 1, k], along(False, k)[1]))
+        return copies
+
+    def rows_of(packed):
+        packed = packed.astype(jnp.float32).reshape(4, 2, 8, QUARTER)
+        low, high = exchange(packed[:, 0], packed[:, 1])
+        return [low.reshape(32, QUARTER), high.reshape(32, QUARTER)]
+
+    def multiply(p, before):
+        for copy in before:
+            copy.wait_recv()
+
+        def scale(zz, carry):
+            place = lax.rem(zz, 2) * 4 + lax.div(zz, 2)
+            quarters = rows_of(ga[p, zz]) + rows_of(gb[p, :, zz])
+            squares = quarters[0] * quarters[0]
+            for part in quarters[1:]:
+                squares = squares + part * part
+            squares = jnp.sum(squares, axis=1, keepdims=True)
+            ssb[p, place] = jnp.sum(jnp.where(diagonal, squares, 0.0), axis=0, keepdims=True)
+            for i, part in enumerate(quarters):
+                lanes = slice(i * QUARTER, (i + 1) * QUARTER)
+                xs[p, place, :, lanes] = (part * gain_ref[:, lanes]).astype(jnp.bfloat16)
+            return carry
+
+        lax.fori_loop(0, N, scale, 0)
+        if p == 0:
+            for load in loads:
+                load.wait()
+        rows = xs[p, pl.ds((1 - c) * 4, 4)].reshape(128, 1024)
+        for start, width in TILES:
+            block = transposed_dot(rows, gu[start : start + width, :])
+            pair_out[p, :, :, start : start + width] = block.astype(jnp.bfloat16).reshape(4, 32, width)
+        pair = [
+            send(pair_out.at[p], pair_in.at[p], ps.at[p, 0], pr.at[p, 0], other),
+            send(ssb.at[p, pl.ds((1 - c) * 4, 4)], pair_ss.at[p], ps.at[p, 1], pr.at[p, 1], other),
+        ]
+        rows = xs[p, pl.ds(c * 4, 4)].reshape(128, 1024)
+        for start, width in TILES:
+            block = transposed_dot(rows, gu[start : start + width, :])
+            own[p, :, :, start : start + width] = block.reshape(4, 32, width)
+        return pair
+
+    def cross(p, before):
+        for copy in before:
+            copy.wait_recv()
+        copies = []
+        for k in (2, 1, 3):
+            xx = past(x, k, NX)
+            x_out[p, k] = (own[p, xx] + pair_in[p, xx].astype(jnp.float32)).astype(jnp.bfloat16)
+            x_ss_out[p, k] = ssb[p, c * 4 + xx] + pair_ss[p, xx]
+            device = at(z, y, xx, c)
+            copies.append(send(x_out.at[p, k], x_in.at[p, k], xsd.at[p, 0, k], xrv.at[p, 0, k], device))
+            copies.append(send(x_ss_out.at[p, k], x_ss_in.at[p, k], xsd.at[p, 1, k], xrv.at[p, 1, k], device))
+        return copies
+
+    def activate(p, before):
+        total = own[p, x] + pair_in[p, x].astype(jnp.float32)
+        squares = ssb[p, c * 4 + x] + pair_ss[p, x]
+        for copy in before:
+            copy.wait_recv()
+        for k in range(1, NX):
+            total = total + x_in[p, k].astype(jnp.float32)
+            squares = squares + x_ss_in[p, k]
+        mean_square = jnp.sum(jnp.where(diagonal, squares, 0.0), axis=1, keepdims=True) / D
+        total = total * lax.rsqrt(mean_square + epsilon)
+        gate = total[:, :512]
+        silu = gate / (1.0 + jnp.exp(-gate))
+        act[p, ffn, :, :MAIN] = (silu[:, :MAIN] * total[:, 512:]).astype(jnp.bfloat16)
+        tail = silu[:, MAIN:] * pltpu.roll(total[:, MAIN:512], 64, 1)
+        act[p, ffn, :, MAIN:] = tail[:, : UNITS - MAIN].astype(jnp.bfloat16)
+        copies = []
+        for k in (2, 1, 3):
+            device = at(z, y, past(x, k, NX), c)
+            copies.append(send(act.at[p, ffn], act.at[p, ffn], acs.at[p, k], acr.at[p, k], device))
+        return copies, [send(act.at[p, ffn], act.at[p, ffn], fws.at[p, 0], fwr.at[p, 0], other)]
+
+    def forward(p, before):
+        copies, passed = before
+        for k, copy in zip((2, 1, 3), copies):
+            copy.wait_recv()
+            block = past(x, NX - k, NX) * 2 + c
+            passed.append(send(act.at[p, block], act.at[p, block], fws.at[p, k], fwr.at[p, k], other))
+        return passed
+
+    def lower(p, before):
+        for copy in before:
+            copy.wait_recv()
+        rows = act[p].reshape(256, UNITS)
+        copies = []
+        for half, (buffer, back) in enumerate(((da, ra), (db, rb))):
+            quarters = [
+                jnp.dot(rows, down[:, start : start + QUARTER], preferred_element_type=jnp.float32)
+                for start in (half * 512, half * 512 + QUARTER)
+            ]
+            low, high = exchange(*[quarter.reshape(32, 8, QUARTER) for quarter in quarters])
+            blocks = jnp.stack([low, high], axis=1).astype(jnp.bfloat16).reshape(N, N, 8, QUARTER)
+            if half == 0:
+                buffer[p] = blocks
+            else:
+                for i in range(N):
+                    buffer[p, :, i] = blocks[i]
+            for k in range(1, N):
+                there, device = along(half == 0, k)
+                copies.append(
+                    send(buffer.at[p, there], back.at[p, k], r1s.at[p, half, k], r1r.at[p, half, k], device)
+                )
+        return copies
+
+    def reduce_second(p, before):
+        copies = []
+        for half, (buffer, back, onward, last) in enumerate(((da, ra, d2a, r2a), (db, rb, d2b, r2b))):
+            here = z if half == 0 else y
+            for copy in before[half * 7 : half * 7 + 7]:
+                copy.wait_recv()
+            added = buffer[p, here].astype(jnp.float32)
+            for k in range(1, N):
+                added = added + back[p, k].astype(jnp.float32)
+            onward[p] = added.astype(jnp.bfloat16)
+            for k in range(1, N):
+                there, device = along(half == 1, k)
+                copies.append(
+                    send(onward.at[p, there], last.at[p, k], r2s.at[p, half, k], r2r.at[p, half, k], device)
+                )
+        return copies
+
+    def finish(p, before):
+        sums = []
+        for half, (onward, last) in enumerate(((d2a, r2a), (d2b, r2b))):
+            here = y if half == 0 else z
+            for copy in before[half * 7 : half * 7 + 7]:
+                copy.wait_recv()
+            added = onward[p, here].astype(jnp.float32)
+            for k in range(1, N):
+                added = added + last[p, k].astype(jnp.float32)
+            sums.append(added)
+        return sums
+
+    first = [gather_first(p) for p in range(PARTS)]
+    second = [gather_second(p, first[p]) for p in range(PARTS)]
+    across = [cross(p, multiply(p, second[p])) for p in range(PARTS)]
+    spread = [forward(p, activate(p, across[p])) for p in range(PARTS)]
+    reduced = [lower(p, spread[p]) for p in range(PARTS)]
+    onward = [reduce_second(p, reduced[p]) for p in range(PARTS)]
+    sums = [finish(p, onward[p]) for p in range(PARTS)]
+    for half in range(2):
+        low, high = exchange(sums[0][half], sums[1][half])
+        out_ref[:, half * 512 : half * 512 + QUARTER] = low
+        out_ref[:, half * 512 + QUARTER : half * 512 + 512] = high
+    for copy in sent:
+        copy.wait_send()
+
+
+def feed_forward(hidden, gain, gate_weight, up_weight, down_weight):
+    bf, f32 = jnp.bfloat16, jnp.float32
+    dma = pltpu.SemaphoreType.DMA
+    vmem = pltpu.VMEM
+    return pl.pallas_call(
+        kernel,
+        out_shape=jax.ShapeDtypeStruct((8, 1024), f32),
+        in_specs=[pl.BlockSpec(memory_space=vmem)] * 2 + [pl.BlockSpec(memory_space=pl.ANY)] * 3,
+        out_specs=pl.BlockSpec(memory_space=vmem),
+        scratch_shapes=[
+            vmem((896, 1024), bf),
+            vmem((UNITS, 1024), bf),
+            vmem((PARTS, N, N, 8, QUARTER), bf),
+            vmem((PARTS, N, N, 8, QUARTER), bf),
+            vmem((PARTS, N, 32, 1024), bf),
+            vmem((PARTS, N, 1, 128), f32),
+            vmem((PARTS, 4, 32, 896), bf),
+            vmem((PARTS, 4, 32, 896), bf),
+            vmem((PARTS, 4, 1, 128), f32),
+            vmem((PARTS, 4, 32, 896), f32),
+            vmem((PARTS, NX, 32, 896), bf),
+            vmem((PARTS, NX, 32, 896), bf),
+            vmem((PARTS, NX, 1, 128), f32),
+            vmem((PARTS, NX, 1, 128), f32),
+            vmem((PARTS, 2 * NX, 32, UNITS), bf),
+            vmem((PARTS, N, N, 8, QUARTER), bf),
+            vmem((PARTS, N, N, 8, QUARTER), bf),
+            vmem((PARTS, N, N, 8, QUARTER), bf),
+            vmem((PARTS, N, N, 8, QUARTER), bf),
+            vmem((PARTS, N, 8, QUARTER), bf),
+            vmem((PARTS, N, 8, QUARTER), bf),
+            vmem((PARTS, N, 8, QUARTER), bf),
+            vmem((PARTS, N, 8, QUARTER), bf),
+            dma((4,)),
+            dma((PARTS, 2, N)),
+            dma((PARTS, 2, N)),
+            dma((PARTS, 2, N)),
+            dma((PARTS, 2, N)),
+            dma((PARTS, 2)),
+            dma((PARTS, 2)),
+            dma((PARTS, 2, NX)),
+            dma((PARTS, 2, NX)),
+            dma((PARTS, NX)),
+            dma((PARTS, NX)),
+            dma((PARTS, NX)),
+            dma((PARTS, NX)),
+            dma((PARTS, 2, N)),
+            dma((PARTS, 2, N)),
+            dma((PARTS, 2, N)),
+            dma((PARTS, 2, N)),
+        ],
+        compiler_params=pltpu.CompilerParams(
+            collective_id=0, has_side_effects=True, vmem_limit_bytes=40 * 1024 * 1024
+        ),
+        cost_estimate=pl.CostEstimate(flops=1_400_000_000, bytes_accessed=3_000_000, transcendentals=0),
+        name="feed_forward",
+    )(hidden, gain, gate_weight, up_weight, down_weight)
 
 
 def on_device(
@@ -64,37 +410,13 @@
 ):
     slot_count = residual.shape[0]
     width_dev = residual.shape[1]
-    units_dev = gate_weight.shape[0]
     attention = attend(queries, cache_keys, cache_values, new_keys, new_values, lengths)
-    attention = lax.optimization_barrier(attention)
     hidden = (residual.astype(jnp.float32) + attention.astype(jnp.float32)).astype(jnp.bfloat16)
-    hidden_f32 = hidden.astype(jnp.float32)
-    square_part = jnp.sum(hidden_f32 * hidden_f32, axis=-1)
-    square_total = lax.psum(square_part, "ffn")
-    mean_square = (square_total / D)[:, None]
     gain_block = lax.dynamic_slice_in_dim(norm_gain, lax.axis_index("ffn") * width_dev, width_dev)
-    outgoing = (
-        hidden_f32 * lax.rsqrt(mean_square + epsilon) * gain_block.astype(jnp.float32)
-    ).astype(jnp.bfloat16)
-    block_rows = lax.all_gather(outgoing, "attn", axis=0, tiled=True)
-    gate_part = lax.dot_general(
-        block_rows, gate_weight, (((1,), (1,)), ((), ())), preferred_element_type=jnp.float32
-    )
-    up_part = lax.dot_general(
-        block_rows, up_weight, (((1,), (1,)), ((), ())), preferred_element_type=jnp.float32
-    )
-    paired = jnp.concatenate([gate_part, up_part], axis=1)
-    summed = lax.psum(paired, "ffn")
-    activated = activate(summed, units_dev)
-    ffn_out = lax.psum_scatter(
-        jnp.dot(activated, down_weight, preferred_element_type=jnp.float32),
-        "attn",
-        scatter_dimension=0,
-        tiled=True,
-    )
-    slot_index = jnp.arange(slot_count, dtype=jnp.int32)
-    is_live = slot_index < counts[0]
-    result = jnp.where(is_live[:, None], hidden_f32 + ffn_out, 0.0)
+    gain = gain_block.astype(jnp.float32)[None, :]
+    ffn_out = feed_forward(hidden, gain, gate_weight, up_weight, down_weight)
+    is_live = jnp.arange(slot_count, dtype=jnp.int32) < counts[0]
+    result = jnp.where(is_live[:, None], hidden.astype(jnp.float32) + ffn_out, 0.0)
     return result.astype(jnp.bfloat16)
 
 

time: 364 us -> 77.2 us (0.21)
  waiting for transfers between devices: 310 us -> 0 us
  Pallas kernels: 0 us -> 69.3 us
  blocking collectives: 18.8 us -> 0 us
  between operations: 14.5 us -> 0.73 us
  matrix products: 9.87 us -> 2.9 us
  other arithmetic: 6.1 us -> 1.67 us
    unnamed x4 -> x0, waiting for transfers between devices: 158 us -> none
    all_gather x1 -> x0, waiting for transfers between devices: 76.6 us -> none  [on_device(): block_rows = lax.all_gather(outgoing, 'attn', axis=0, tiled=True)]
    psum x1 -> x0, waiting for transfers between devices: 75.3 us -> none  [on_device(): summed = lax.psum(paired, 'ffn')]
    pallas_call x0 -> x1, Pallas kernels: none -> 69.3 us  [feed_forward(): pl.pallas_call(kernel, out_shape=jax.ShapeDtypeStruct((8, 1024), f32), in...]
    psum x1 -> x0, blocking collectives: 18.8 us -> none  [on_device(): square_total = lax.psum(square_part, 'ffn')]
    dot_general x3 -> x0, matrix products: 6.34 us -> none  [the longest x1 3.59 us: on_device(): jnp.dot(activated, down_weight, preferred_element_type=jnp.float32)]
  transfers between devices with their start and end apart: 3 -> 0, of which waited for: 3 -> 0; matrix products, arithmetic and copies ran while one was open for 0% -> 0% of each run, Pallas kernels for 0% -> 0%
where the time goes in v2:
time: 77.2 us; the launch traced here: 77 us
  Pallas kernels  69.3 us (90%)
  matrix products  2.9 us (4%)
  local copies, waits for them, and re-layouts  2.37 us (3%)
  other arithmetic  1.67 us (2%)
    pallas_call x1, Pallas kernels, feed_forward(): pl.pallas_call(kernel, out_shape=jax.ShapeDtypeStruct((8, 1024), f32), in...  69.3 us
    unnamed x18, local copies, waits for them, and re-layouts  2.37 us

profile of v2, /device:TPU:1, one launch (start us, length us, event | category | flops | bytes accessed | tf_op | source)
XLA Modules:
  0.0 77.0 jit_solution(17590091713279801141)
XLA Ops:
  0.0 0.0 copy-start
  0.0 0.0 copy-start.7
  0.0 0.7 copy-done.7
  0.7 0.1 iota_compare_fusion
  0.8 0.4 copy-done
  1.2 0.0 copy-start.4
  1.2 0.0 copy-start.8
  1.2 0.0 copy-start.6
  1.2 0.0 copy-start.2
  1.3 1.3 %fusion.16 = (f32[8,8]{1,0:T(8,128)S(1)}, f32[8,8,512]{2,1,0:T(8,128)S(1)}) fusion(bf16[8,1,512,128]{3,2,1,0:T(8,128)(2,1)S(1)} %copy-done, bf16[8,8,128]{2,0,1:T(8,128)(2,1)} %bitcast.26, pred[8,512]{1,0:T(8,128)(4,1)S(1)} %iota_compare_fusion), kind=kOutput, calls=%fused_computation.29 | convolution fusion | flops 8486848 | bytes 1200384 | tf_op jit(solution)/shard_map/rgqd,rgpd->rgqp/dot_general | solution.py:23
  2.5 0.0 copy-start.1
  2.5 0.0 copy-done.4
  2.5 0.0 copy-done.8
  2.5 0.1 fusion.10
  2.7 0.2 fusion.6
  2.9 0.0 copy-done.6
  2.9 0.0 copy-start.5
  2.9 1.5 %fusion.3 = f32[1,8,8,128]{3,2,1,0:T(8,128)S(1)} fusion(bf16[8,1,512,128]{3,2,1,0:T(8,128)(2,1)} %param.15, f32[8,8,512]{2,1,0:T(8,128)S(1)} %get-tuple-element.8, f32[8,8]{1,0:T(8,128)S(1)} %get-tuple-element.6, f32[8,8]{1,0:T(8,128)S(1)} %multiply_maximum_fusion, f32[8,128]{1,0:T(8,128)S(1)} %bitcast_convert_fusion, f32[8,8]{1,0:T(8,128)S(1)} %get-tuple-element.5), kind=kOutput, calls=%fused_computation.5 | convolution fusion | flops 8519680 | bytes 1217280 | tf_op jit(solution)/shard_map/rgqp,rgpd->rgqd/dot_general | solution.py:39
  4.4 0.0 copy-done.5
  4.4 0.7 dynamic-slice_convert_fusion
  5.1 0.0 copy-done.2
  5.1 0.0 copy-done.1
  5.1 0.0 copy-start.3
  5.1 1.2 %copy-done.3 = bf16[448,1024]{1,0:T(8,128)(2,1)S(1)} copy-done((bf16[448,1024]{1,0:T(8,128)(2,1)S(1)}, bf16[448,1024]{1,0:T(8,128)(2,1)}, u32[]{:S(2)}) %copy-start.3) | copy-done | bytes 917528
  6.3 69.3 %feed_forward.1 = f32[8,1024]{1,0:T(8,128)S(1)} custom-call(bf16[8,1024]{1,0:T(8,128)(2,1)S(1)} %fusion.9.hidden_ref, f32[1,1024]{1,0:T(1,128)S(1)} %bitcast.25, bf16[448,1024]{1,0:T(8,128)(2,1)S(1)} %copy-done.1, bf16[448,1024]{1,0:T(8,128)(2,1)S(1)} %copy-done.2, bf16[448,1024]{1,0:T(8,128)(2,1)S(1)} %copy-done.3), custom_call_target="tpu_custom_call" | custom-call | flops 1400000000 | bytes 3000000 | tf_op jit(solution)/shard_map/feed_forward/pallas_call | solution.py:342
  76.3 0.7 select_convert_fusion
  (5 shorter events, 0.0 us)
Async XLA Ops:
  0.0 1.2 %copy-start = (bf16[8,1,512,128]{3,2,1,0:T(8,128)(2,1)S(1)}, bf16[8,1,512,128]{3,2,1,0:T(8,128)(2,1)}, u32[]{:S(2)}) copy-start(bf16[8,1,512,128]{3,2,1,0:T(8,128)(2,1)} %param.14) | copy-start | bytes 3145732
  0.0 0.7 copy-start.7
  1.2 1.3 %copy-start.4 = (bf16[8,1024]{1,0:T(8,128)(2,1)S(1)}, bf16[8,1024]{1,0:T(8,128)(2,1)}, u32[]{:S(2)}) copy-start(bf16[8,1024]{1,0:T(8,128)(2,1)} %param.13) | copy-start | bytes 49156
  1.2 1.3 %copy-start.8 = (bf16[8,1,128]{2,0,1:T(8,128)(2,1)S(1)}, bf16[8,1,128]{2,0,1:T(8,128)(2,1)}, u32[]{:S(2)}) copy-start(bf16[8,1,128]{2,0,1:T(8,128)(2,1)} %param.16) | copy-start | bytes 6148
  1.2 1.6 %copy-start.6 = (bf16[8,1,128]{2,0,1:T(8,128)(2,1)S(1)}, bf16[8,1,128]{2,0,1:T(8,128)(2,1)}, u32[]{:S(2)}) copy-start(bf16[8,1,128]{2,0,1:T(8,128)(2,1)} %param.17) | copy-start | bytes 6148
  1.2 3.9 %copy-start.2 = (bf16[448,1024]{1,0:T(8,128)(2,1)S(1)}, bf16[448,1024]{1,0:T(8,128)(2,1)}, u32[]{:S(2)}) copy-start(bf16[448,1024]{1,0:T(8,128)(2,1)} %up_hbm.1) | copy-start | bytes 2752516
  2.5 2.6 %copy-start.1 = (bf16[448,1024]{1,0:T(8,128)(2,1)S(1)}, bf16[448,1024]{1,0:T(8,128)(2,1)}, u32[]{:S(2)}) copy-start(bf16[448,1024]{1,0:T(8,128)(2,1)} %gate_hbm.1) | copy-start | bytes 2752516
  2.9 1.5 %copy-start.5 = (bf16[8,1024]{1,0:T(8,128)(2,1)S(1)}, bf16[8,1024]{1,0:T(8,128)(2,1)}, u32[]{:S(2)}) copy-start(bf16[8,1024]{1,0:T(8,128)(2,1)} %param.12) | copy-start | bytes 49156
  5.1 1.2 %copy-start.3 = (bf16[448,1024]{1,0:T(8,128)(2,1)S(1)}, bf16[448,1024]{1,0:T(8,128)(2,1)}, u32[]{:S(2)}) copy-start(bf16[448,1024]{1,0:T(8,128)(2,1)} %down_hbm.1) | copy-start | bytes 2752516

commit v3 on v2

--- a/solution.py
+++ b/solution.py
@@ -9,41 +9,6 @@
 
 
 epsilon = 1e-05
-
-
-def attend(queries, cache_keys, cache_values, new_keys, new_values, lengths):
-    slot_count = queries.shape[0]
-    kv_dev = cache_keys.shape[1]
-    ctx_len = cache_keys.shape[2]
-    head_dim = cache_keys.shape[3]
-    head_group = queries.shape[1] // (kv_dev * head_dim)
-    score_scale = 1.0 / head_dim**0.5
-    query_heads = queries.reshape(slot_count, kv_dev, head_group, head_dim)
-    scores = (
-        jnp.einsum("rgqd,rgpd->rgqp", query_heads, cache_keys, preferred_element_type=jnp.float32)
-        * score_scale
-    )
-    positions = jnp.arange(ctx_len, dtype=jnp.int32)
-    allowed = positions[None, None, None, :] < lengths[:, None, None, None]
-    scores = jnp.where(allowed, scores, -1e30)
-    own_score = (
-        jnp.einsum("rgqd,rgd->rgq", query_heads, new_keys, preferred_element_type=jnp.float32)
-        * score_scale
-    )
-    row_max = jnp.maximum(jnp.max(scores, axis=-1), own_score)
-    key_weights = jnp.exp(scores - row_max[..., None])
-    own_weight = jnp.exp(own_score - row_max)
-    denominator = jnp.sum(key_weights, axis=-1) + own_weight
-    key_probs = (key_weights / denominator[..., None]).astype(jnp.bfloat16)
-    own_prob = (own_weight / denominator).astype(jnp.bfloat16)
-    mixed = jnp.einsum(
-        "rgqp,rgpd->rgqd", key_probs, cache_values, preferred_element_type=jnp.float32
-    )
-    mixed = (
-        mixed
-        + own_prob.astype(jnp.float32)[..., None] * new_values.astype(jnp.float32)[:, :, None, :]
-    )
-    return mixed.reshape(slot_count, kv_dev * head_group * head_dim).astype(jnp.bfloat16)
 
 
 MESH = pl.DeviceIdType.MESH
@@ -66,13 +31,79 @@
     return jnp.where(upper, low, pltpu.roll(high, 4, axis)), jnp.where(upper, pltpu.roll(low, 4, axis), high)
 
 
+def attend(
+    inputs,
+    queries_ref,
+    keys_ref,
+    values_ref,
+    new_keys_ref,
+    new_values_ref,
+    lengths_ref,
+    residual_ref,
+    by_head,
+    hidden_ref,
+):
+    for load in inputs[:4]:
+        load.wait()
+    score_scale = 1.0 / 128**0.5
+    for h in range(8):
+        by_head[h * 8 : h * 8 + 8, :] = queries_ref[:, h * 128 : h * 128 + 128].astype(jnp.float32)
+    new_keys = new_keys_ref[...].astype(jnp.float32)
+    position = lax.broadcasted_iota(jnp.int32, (8, 512), 1)
+    scores = []
+    own = []
+    for r in range(8):
+        query = by_head[pl.ds(r, 8, stride=8), :]
+        own.append(jnp.sum(query * new_keys[r : r + 1, :], axis=1, keepdims=True))
+        slot = transposed_dot(query.astype(jnp.bfloat16), keys_ref[r]) * score_scale
+        scores.append(jnp.where(position < lengths_ref[r], slot, -1e30))
+    scores = jnp.concatenate(scores, axis=0)
+    own = jnp.concatenate(own, axis=0) * score_scale
+    row_max = jnp.maximum(jnp.max(scores, axis=1, keepdims=True), own)
+    key_weights = jnp.exp(scores - row_max)
+    own_weight = jnp.exp(own - row_max)
+    denominator = jnp.sum(key_weights, axis=1, keepdims=True) + own_weight
+    key_probs = key_weights / denominator
+    own_prob = (own_weight / denominator).astype(jnp.bfloat16).astype(jnp.float32)
+    for load in inputs[4:]:
+        load.wait()
+    new_values = new_values_ref[...].astype(jnp.float32)
+    for r in range(8):
+        probs = key_probs[r * 8 : r * 8 + 8, :].astype(jnp.bfloat16)
+        mixed = jnp.dot(probs, values_ref[r], preferred_element_type=jnp.float32)
+        mixed = mixed + own_prob[r * 8 : r * 8 + 8, :] * new_values[r : r + 1, :]
+        by_head[pl.ds(r, 8, stride=8), :] = mixed.astype(jnp.bfloat16).astype(jnp.float32)
+    for h in range(8):
+        lanes = slice(h * 128, h * 128 + 128)
+        hidden = residual_ref[:, lanes].astype(jnp.float32) + by_head[h * 8 : h * 8 + 8, :]
+        hidden_ref[:, lanes] = hidden.astype(jnp.bfloat16).astype(jnp.float32)
+
+
 def kernel(
-    hidden_ref,
-    gain_ref,
+    residual_hbm,
+    queries_hbm,
+    keys_hbm,
+    values_hbm,
+    new_keys_hbm,
+    new_values_hbm,
+    lengths_hbm,
+    counts_hbm,
+    gain_hbm,
     gate_hbm,
     up_hbm,
     down_hbm,
     out_ref,
+    residual_ref,
+    queries_ref,
+    keys_ref,
+    values_ref,
+    new_keys_ref,
+    new_values_ref,
+    lengths_ref,
+    counts_ref,
+    gain_ref,
+    by_head,
+    hidden_ref,
     gu,
     down,
     ga,
@@ -96,6 +127,7 @@
     d2b,
     r2a,
     r2b,
+    asem,
     wsem,
     g1s,
     g1r,
@@ -125,6 +157,24 @@
     def past(i, k, n):
         return lax.rem(i + k, n)
 
+    inputs = [
+        pltpu.make_async_copy(source, target, asem.at[i])
+        for i, (source, target) in enumerate(
+            (
+                (queries_hbm, queries_ref),
+                (new_keys_hbm, new_keys_ref),
+                (lengths_hbm, lengths_ref),
+                (keys_hbm, keys_ref),
+                (values_hbm, values_ref),
+                (new_values_hbm, new_values_ref),
+                (residual_hbm, residual_ref),
+                (counts_hbm, counts_ref),
+                (gain_hbm.at[pl.ds(ffn * 1024, 1024)], gain_ref),
+            )
+        )
+    ]
+    for load in inputs:
+        load.start()
     loads = [
         pltpu.make_async_copy(gate_hbm, gu.at[pl.ds(0, UNITS)], wsem.at[0]),
         pltpu.make_async_copy(up_hbm.at[pl.ds(MAIN, UNITS - MAIN)], gu.at[pl.ds(UNITS, UNITS - MAIN)], wsem.at[1]),
@@ -141,6 +191,20 @@
     partners += [at(z, y, x, 1 - c)]
     for partner in partners:
         pl.semaphore_signal(barrier, inc=1, device_id=partner, device_id_type=MESH)
+
+    attend(
+        inputs,
+        queries_ref,
+        keys_ref,
+        values_ref,
+        new_keys_ref,
+        new_values_ref,
+        lengths_ref,
+        residual_ref,
+        by_head,
+        hidden_ref,
+    )
+    gain = gain_ref[...].astype(jnp.float32).reshape(1, 1024)
     pl.semaphore_wait(barrier, len(partners))
 
     sent = []
@@ -163,7 +227,7 @@
             return past(z, k, N), at(past(z, k, N), y, x, c)
         return past(y, k, N), at(z, past(y, k, N), x, c)
 
-    wide = hidden_ref[...].astype(jnp.float32)
+    wide = hidden_ref[...]
     for buffer, start, one, two in ((ga, 0, z, y), (gb, 512, y, z)):
         blocks = exchange(wide[:, start : start + QUARTER], wide[:, start + QUARTER : start + 512])
         for p in range(PARTS):
@@ -204,7 +268,7 @@
             ssb[p, place] = jnp.sum(jnp.where(diagonal, squares, 0.0), axis=0, keepdims=True)
             for i, part in enumerate(quarters):
                 lanes = slice(i * QUARTER, (i + 1) * QUARTER)
-                xs[p, place, :, lanes] = (part * gain_ref[:, lanes]).astype(jnp.bfloat16)
+                xs[p, place, :, lanes] = (part * gain[:, lanes]).astype(jnp.bfloat16)
             return carry
 
         lax.fori_loop(0, N, scale, 0)
@@ -327,24 +391,36 @@
     reduced = [lower(p, spread[p]) for p in range(PARTS)]
     onward = [reduce_second(p, reduced[p]) for p in range(PARTS)]
     sums = [finish(p, onward[p]) for p in range(PARTS)]
+    live = lax.broadcasted_iota(jnp.int32, (8, QUARTER), 0) < counts_ref[0]
     for half in range(2):
-        low, high = exchange(sums[0][half], sums[1][half])
-        out_ref[:, half * 512 : half * 512 + QUARTER] = low
-        out_ref[:, half * 512 + QUARTER : half * 512 + 512] = high
+        for i, part in enumerate(exchange(sums[0][half], sums[1][half])):
+            lanes = slice(half * 512 + i * QUARTER, half * 512 + (i + 1) * QUARTER)
+            out_ref[:, lanes] = jnp.where(live, hidden_ref[:, lanes] + part, 0.0).astype(jnp.bfloat16)
     for copy in sent:
         copy.wait_send()
 
 
-def feed_forward(hidden, gain, gate_weight, up_weight, down_weight):
+def whole_layer(*operands):
     bf, f32 = jnp.bfloat16, jnp.float32
     dma = pltpu.SemaphoreType.DMA
     vmem = pltpu.VMEM
     return pl.pallas_call(
         kernel,
-        out_shape=jax.ShapeDtypeStruct((8, 1024), f32),
-        in_specs=[pl.BlockSpec(memory_space=vmem)] * 2 + [pl.BlockSpec(memory_space=pl.ANY)] * 3,
+        out_shape=jax.ShapeDtypeStruct((8, 1024), bf),
+        in_specs=[pl.BlockSpec(memory_space=pltpu.HBM)] * 12,
         out_specs=pl.BlockSpec(memory_space=vmem),
         scratch_shapes=[
+            vmem((8, 1024), bf),
+            vmem((8, 1024), bf),
+            vmem((8, 512, 128), bf),
+            vmem((8, 512, 128), bf),
+            vmem((8, 128), bf),
+            vmem((8, 128), bf),
+            pltpu.SMEM((8,), jnp.int32),
+            pltpu.SMEM((1,), jnp.int32),
+            vmem((1024,), bf),
+            vmem((64, 128), f32),
+            vmem((8, 1024), f32),
             vmem((896, 1024), bf),
             vmem((UNITS, 1024), bf),
             vmem((PARTS, N, N, 8, QUARTER), bf),
@@ -368,6 +444,7 @@
             vmem((PARTS, N, 8, QUARTER), bf),
             vmem((PARTS, N, 8, QUARTER), bf),
             vmem((PARTS, N, 8, QUARTER), bf),
+            dma((9,)),
             dma((4,)),
             dma((PARTS, 2, N)),
             dma((PARTS, 2, N)),
@@ -387,11 +464,11 @@
             dma((PARTS, 2, N)),
         ],
         compiler_params=pltpu.CompilerParams(
-            collective_id=0, has_side_effects=True, vmem_limit_bytes=40 * 1024 * 1024
+            collective_id=0, has_side_effects=True, vmem_limit_bytes=60 * 1024 * 1024
         ),
-        cost_estimate=pl.CostEstimate(flops=1_400_000_000, bytes_accessed=3_000_000, transcendentals=0),
-        name="feed_forward",
-    )(hidden, gain, gate_weight, up_weight, down_weight)
+        cost_estimate=pl.CostEstimate(flops=1_430_000_000, bytes_accessed=5_000_000, transcendentals=0),
+        name="whole_layer",
+    )(*operands)
 
 
 def on_device(
@@ -408,16 +485,20 @@
     up_weight,
     down_weight,
 ):
-    slot_count = residual.shape[0]
-    width_dev = residual.shape[1]
-    attention = attend(queries, cache_keys, cache_values, new_keys, new_values, lengths)
-    hidden = (residual.astype(jnp.float32) + attention.astype(jnp.float32)).astype(jnp.bfloat16)
-    gain_block = lax.dynamic_slice_in_dim(norm_gain, lax.axis_index("ffn") * width_dev, width_dev)
-    gain = gain_block.astype(jnp.float32)[None, :]
-    ffn_out = feed_forward(hidden, gain, gate_weight, up_weight, down_weight)
-    is_live = jnp.arange(slot_count, dtype=jnp.int32) < counts[0]
-    result = jnp.where(is_live[:, None], hidden.astype(jnp.float32) + ffn_out, 0.0)
-    return result.astype(jnp.bfloat16)
+    return whole_layer(
+        residual,
+        queries,
+        cache_keys.reshape(8, 512, 128),
+        cache_values.reshape(8, 512, 128),
+        new_keys.reshape(8, 128),
+        new_values.reshape(8, 128),
+        lengths,
+        counts,
+        norm_gain,
+        gate_weight,
+        up_weight,
+        down_weight,
+    )
 
 
 def solution(mesh):

time: 77.2 us -> 71.5 us (0.926)
  matrix products: 2.9 us -> 0 us
  other arithmetic: 1.67 us -> 0 us
  local copies, waits for them, and re-layouts: 2.37 us -> 1.32 us
    dot_general x3 -> x0, matrix products: 2.9 us -> none  [the longest x1 1.53 us: attend(): jnp.einsum('rgqp,rgpd->rgqd', key_probs, cache_values, preferred_element_...]
    unnamed x18 -> x1, local copies, waits for them, and re-layouts: 2.37 us -> 1.32 us
where the time goes in v3:
time: 71.5 us; the launch traced here: 70.6 us
  Pallas kernels  68.6 us (96%)
  local copies, waits for them, and re-layouts  1.32 us (2%)
    pallas_call x1, Pallas kernels, whole_layer(): pl.pallas_call(kernel, out_shape=jax.ShapeDtypeStruct((8, 1024), bf), in_...  68.6 us

profile of v3, /device:TPU:1, one launch (start us, length us, event | category | flops | bytes accessed | tf_op | source)
XLA Modules:
  0.0 70.6 jit_solution(310974902380697986)
XLA Ops:
  0.7 68.6 %whole_layer.1 = bf16[8,1024]{1,0:T(8,128)(2,1)} custom-call(bf16[8,1024]{1,0:T(8,128)(2,1)} %residual_hbm.1, bf16[8,1024]{1,0:T(8,128)(2,1)} %queries_hbm.1, bf16[8,512,128]{2,1,0:T(8,128)(2,1)} %bitcast.4, bf16[8,512,128]{2,1,0:T(8,128)(2,1)} %bitcast.5, bf16[8,128]{1,0:T(8,128)(2,1)} %bitcast.6, bf16[8,128]{1,0:T(8,128)(2,1)} %bitcast.7, s32[8]{0:T(128)} %lengths_hbm.1, ...), custom_call_target="tpu_custom_call" | custom-call | flops 1430000000 | bytes 5000000 | tf_op jit(solution)/shard_map/whole_layer/pallas_call | solution.py:407
  69.2 1.3 %copy.15 = bf16[8,1024]{1,0:T(8,128)(2,1)} copy(bf16[8,1024]{1,0:T(8,128)(2,1)} %whole_layer.1) | data formatting | bytes 32768

commit v4 on v3

v4 whole, which is shorter than its diff:
```python
import jax
import jax.numpy as jnp
from jax import lax
from jax.experimental import pallas as pl
from jax.experimental.pallas import tpu as pltpu
from jax.sharding import PartitionSpec as P

D = 8192


epsilon = 1e-05


MESH = pl.DeviceIdType.MESH
N = 8
NX = 4
HALF = 512
UNITS = 448
MAIN = 384
TILES = ((0, 256), (256, 256), (512, 256), (768, 128))
STEPS = (0, 1, -1, 2, -2, 3, -3, 4)
GROUPS = ((0, 1, 2, 3, 4), (5, 6, 7))


def transposed_dot(rows, weight):
    return lax.dot_general(rows, weight, (((1,), (1,)), ((), ())), preferred_element_type=jnp.float32)


def exchange(low, high):
    axis = low.ndim - 2
    upper = lax.broadcasted_iota(jnp.int32, low.shape, axis) < 4
    return jnp.where(upper, low, pltpu.roll(high, 4, axis)), jnp.where(upper, pltpu.roll(low, 4, axis), high)


def attend(
    inputs,
    queries_ref,
    keys_ref,
    values_ref,
    new_keys_ref,
    new_values_ref,
    lengths_ref,
    residual_ref,
    by_head,
    hidden_ref,
):
    for load in inputs[:4]:
        load.wait()
    score_scale = 1.0 / 128**0.5
    for h in range(8):
        by_head[h * 8 : h * 8 + 8, :] = queries_ref[:, h * 128 : h * 128 + 128].astype(jnp.float32)
    new_keys = new_keys_ref[...].astype(jnp.float32)
    position = lax.broadcasted_iota(jnp.int32, (8, 512), 1)
    scores = []
    own = []
    for r in range(8):
        query = by_head[pl.ds(r, 8, stride=8), :]
        own.append(jnp.sum(query * new_keys[r : r + 1, :], axis=1, keepdims=True))
        slot = transposed_dot(query.astype(jnp.bfloat16), keys_ref[r]) * score_scale
        scores.append(jnp.where(position < lengths_ref[r], slot, -1e30))
    scores = jnp.concatenate(scores, axis=0)
    own = jnp.concatenate(own, axis=0) * score_scale
    row_max = jnp.maximum(jnp.max(scores, axis=1, keepdims=True), own)
    key_weights = jnp.exp(scores - row_max)
    own_weight = jnp.exp(own - row_max)
    denominator = jnp.sum(key_weights, axis=1, keepdims=True) + own_weight
    key_probs = key_weights / denominator
    own_prob = (own_weight / denominator).astype(jnp.bfloat16).astype(jnp.float32)
    for load in inputs[4:]:
        load.wait()
    new_values = new_values_ref[...].astype(jnp.float32)
    for r in range(8):
        probs = key_probs[r * 8 : r * 8 + 8, :].astype(jnp.bfloat16)
        mixed = jnp.dot(probs, values_ref[r], preferred_element_type=jnp.float32)
        mixed = mixed + own_prob[r * 8 : r * 8 + 8, :] * new_values[r : r + 1, :]
        by_head[pl.ds(r, 8, stride=8), :] = mixed.astype(jnp.bfloat16).astype(jnp.float32)
    for h in range(8):
        lanes = slice(h * 128, h * 128 + 128)
        hidden = residual_ref[:, lanes].astype(jnp.float32) + by_head[h * 8 : h * 8 + 8, :]
        hidden_ref[:, lanes] = hidden.astype(jnp.bfloat16).astype(jnp.float32)


def kernel(
    residual_hbm,
    queries_hbm,
    keys_hbm,
    values_hbm,
    new_keys_hbm,
    new_values_hbm,
    lengths_hbm,
    counts_hbm,
    gain_hbm,
    gate_hbm,
    up_hbm,
    down_hbm,
    out_ref,
    residual_ref,
    queries_ref,
    keys_ref,
    values_ref,
    new_keys_ref,
    new_values_ref,
    lengths_ref,
    counts_ref,
    gain_ref,
    by_head,
    hidden_ref,
    gu,
    down,
    held,
    terms,
    back,
    onward,
    last,
    asem,
    wsem,
    g1s,
    g1r,
    g2s,
    g2r,
    r1s,
    r1r,
    r2s,
    r2r,
    *by_group,
):
    each = len(by_group) // len(GROUPS)
    by_group = [by_group[g * each : g * each + each] for g in range(len(GROUPS))]
    attn = lax.axis_index("attn")
    ffn = lax.axis_index("ffn")
    z, y = lax.div(attn, N), lax.rem(attn, N)
    x, c = lax.div(ffn, 2), lax.rem(ffn, 2)

    def at(zz, yy, xx, cc):
        return (zz * N + yy, xx * 2 + cc)

    def past(i, k, n):
        return lax.rem(i + k, n)

    inputs = [
        pltpu.make_async_copy(source, target, asem.at[i])
        for i, (source, target) in enumerate(
            (
                (queries_hbm, queries_ref),
                (new_keys_hbm, new_keys_ref),
                (lengths_hbm, lengths_ref),
                (keys_hbm, keys_ref),
                (values_hbm, values_ref),
                (new_values_hbm, new_values_ref),
                (residual_hbm, residual_ref),
                (counts_hbm, counts_ref),
                (gain_hbm.at[pl.ds(ffn * 1024, 1024)], gain_ref),
            )
        )
    ]
    for load in inputs:
        load.start()
    loads = [
        pltpu.make_async_copy(gate_hbm, gu.at[pl.ds(0, UNITS)], wsem.at[0]),
        pltpu.make_async_copy(up_hbm.at[pl.ds(MAIN, UNITS - MAIN)], gu.at[pl.ds(UNITS, UNITS - MAIN)], wsem.at[1]),
        pltpu.make_async_copy(up_hbm.at[pl.ds(0, MAIN)], gu.at[pl.ds(512, MAIN)], wsem.at[2]),
        pltpu.make_async_copy(down_hbm, down, wsem.at[3]),
    ]
    for load in loads:
        load.start()

    barrier = pltpu.get_barrier_semaphore()
    partners = [at(past(z, k, N), y, x, c) for k in range(1, N)]
    partners += [at(z, past(y, k, N), x, c) for k in range(1, N)]
    partners += [at(z, y, past(x, k, NX), c) for k in range(1, NX)]
    partners += [at(z, y, x, 1 - c)]
    for partner in partners:
        pl.semaphore_signal(barrier, inc=1, device_id=partner, device_id_type=MESH)

    attend(
        inputs,
        queries_ref,
        keys_ref,
        values_ref,
        new_keys_ref,
        new_values_ref,
        lengths_ref,
        residual_ref,
        by_head,
        hidden_ref,
    )
    gain = gain_ref[...].astype(jnp.float32).reshape(1, 1024)
    pl.semaphore_wait(barrier, len(partners))

    sent = []

    def send(source, target, send_sem, recv_sem, device):
        copy = pltpu.make_async_remote_copy(
            src_ref=source, dst_ref=target, send_sem=send_sem, recv_sem=recv_sem, device_id=device, device_id_type=MESH
        )
        copy.start()
        sent.append(copy)
        return copy

    other = at(z, y, x, 1 - c)

    def along(is_z, step):
        if is_z:
            return at(lax.rem(z + (N + step), N), y, x, c)
        return at(z, lax.rem(y + (N + step), N), x, c)

    blocks = exchange(hidden_ref[:, :HALF], hidden_ref[:, HALF:])
    first, second = [[], []], [{}, {}]
    for route in range(2):
        held[route, 0, 0] = blocks[route].astype(jnp.bfloat16)
    for i in (7, 5, 6, 3, 4, 1, 2):
        for route in range(2):
            first[route].append(
                send(
                    held.at[route, 0, 0],
                    held.at[route, 0, i],
                    g1s.at[route, i],
                    g1r.at[route, i],
                    along(route == 1, -STEPS[i]),
                )
            )

    def pass_on(route, i, source, device):
        second[route][i] = send(
            held.at[route, source], held.at[route, i], g2s.at[route, i], g2r.at[route, i], device
        )

    for route in range(2):
        for copy in first[route]:
            copy.wait_recv()
        for i in (3, 4, 1, 2):
            pass_on(route, i, 0, along(route == 0, -STEPS[i]))
    for route in range(2):
        second[route][3].wait_recv()
        second[route][4].wait_recv()
        pass_on(route, 7, 3 + c, along(route == 0, -2 + 4 * c))
        pass_on(route, 5, 3, along(route == 0, -1))
        pass_on(route, 6, 4, along(route == 0, 1))

    def multiply(g):
        xs, ssb, pair_out, pair_in, pair_ss, own = by_group[g][:6]
        places = GROUPS[g]
        count = len(places)
        lane = lax.broadcasted_iota(jnp.int32, (4, 8, 128), 2)
        row = lax.broadcasted_iota(jnp.int32, (4, 8, 128), 1)
        for route in range(2):
            squares = jnp.zeros((4, 1, 128), jnp.float32)
            for d, i in enumerate(places):
                if i in (1, 2, 5, 6, 7):
                    second[route][i].wait_recv()
                packed = held[route, i].astype(jnp.float32).reshape(4, 2, 8, HALF)
                low, high = exchange(packed[:, 0], packed[:, 1])
                square = jnp.sum(low * low + high * high, axis=2, keepdims=True)
                squares = squares + jnp.sum(jnp.where(lane == row + 8 * d, square, 0.0), axis=1, keepdims=True)
                xs[route * 4 : route * 4 + 4, d, :, :HALF] = (low * gain[:, :HALF]).astype(jnp.bfloat16)
                xs[route * 4 : route * 4 + 4, d, :, HALF:] = (high * gain[:, HALF:]).astype(jnp.bfloat16)
            ssb[route * 4 : route * 4 + 4] = squares
        if g == 0:
            for load in loads:
                load.wait()
        rows = xs[pl.ds((1 - c) * 4, 4)].reshape(32 * count, 1024)
        for start, width in TILES:
            block = transposed_dot(rows, gu[start : start + width, :]).astype(jnp.bfloat16)
            pair_out[:, :, :, start : start + width] = block.reshape(4, count, 8, width)
        pair = [
            send(pair_out, pair_in, by_group[g][11].at[0], by_group[g][12].at[0], other),
            send(ssb.at[pl.ds((1 - c) * 4, 4)], pair_ss, by_group[g][11].at[1], by_group[g][12].at[1], other),
        ]
        rows = xs[pl.ds(c * 4, 4)].reshape(32 * count, 1024)
        for start, width in TILES:
            block = transposed_dot(rows, gu[start : start + width, :])
            own[:, :, :, start : start + width] = block.reshape(4, count, 8, width)
        return pair

    def cross(g, before):
        ssb, _, pair_in, pair_ss, own, x_out, x_in, x_ss_out, x_ss_in = by_group[g][1:10]
        xss, xsr = by_group[g][13:15]
        for copy in before:
            copy.wait_recv()
        copies = []
        for k in (2, 1, 3):
            xx = past(x, k, NX)
            x_out[k] = (own[xx] + pair_in[xx].astype(jnp.float32)).astype(jnp.bfloat16)
            x_ss_out[k] = ssb[c * 4 + xx] + pair_ss[xx]
            device = at(z, y, xx, c)
            copies.append(send(x_out.at[k], x_in.at[k], xss.at[0, k], xsr.at[0, k], device))
            copies.append(send(x_ss_out.at[k], x_ss_in.at[k], xss.at[1, k], xsr.at[1, k], device))
        return copies

    def activate(g, before):
        ssb, _, pair_in, pair_ss, own, _, x_in, _, x_ss_in, act = by_group[g][1:11]
        acs, acr, fws, fwr = by_group[g][15:19]
        count = len(GROUPS[g])
        total = own[x] + pair_in[x].astype(jnp.float32)
        squares = ssb[c * 4 + x] + pair_ss[x]
        for copy in before:
            copy.wait_recv()
        for k in range(1, NX):
            total = total + x_in[k].astype(jnp.float32)
            squares = squares + x_ss_in[k]
        total = total.reshape(8 * count, 896)
        lane = lax.broadcasted_iota(jnp.int32, (8 * count, 128), 1)
        row = lax.broadcasted_iota(jnp.int32, (8 * count, 128), 0)
        mean_square = jnp.sum(jnp.where(lane == row, squares, 0.0), axis=1, keepdims=True) / D
        total = total * lax.rsqrt(mean_square + epsilon)
        gate = total[:, :512]
        silu = gate / (1.0 + jnp.exp(-gate))
        mine = c * 4 + x
        main = (silu[:, :MAIN] * total[:, 512:]).astype(jnp.bfloat16)
        act[mine, :, :, :MAIN] = main.reshape(count, 8, MAIN)
        tail = (silu[:, MAIN:] * pltpu.roll(total[:, MAIN:512], 64, 1))[:, : UNITS - MAIN]
        act[mine, :, :, MAIN:] = tail.astype(jnp.bfloat16).reshape(count, 8, UNITS - MAIN)
        copies = []
        for k in (2, 1, 3):
            device = at(z, y, past(x, k, NX), c)
            copies.append(send(act.at[mine], act.at[mine], acs.at[k], acr.at[k], device))
        return copies, [send(act.at[mine], act.at[mine], fws.at[0], fwr.at[0], other)]

    def forward(g, before):
        act = by_group[g][10]
        fws, fwr = by_group[g][17:19]
        copies, passed = before
        for k, copy in zip((1, 3, 2), (copies[1], copies[2], copies[0])):
            copy.wait_recv()
            place = c * 4 + past(x, NX - k, NX)
            passed.append(send(act.at[place], act.at[place], fws.at[k], fwr.at[k], other))
        return passed

    reduced = [{}, {}]

    def lower(g, before):
        act = by_group[g][10]
        places = GROUPS[g]
        count = len(places)
        for copy in before:
            copy.wait_recv()
        rows = act[...].reshape(64 * count, UNITS)
        for start in (0, 256):
            quarters = [
                jnp.dot(rows, down[:, at_lane : at_lane + 256], preferred_element_type=jnp.float32)
                for at_lane in (start, start + HALF)
            ]
            halves = exchange(*[quarter.reshape(2, 4, count, 8, 256) for quarter in quarters])
            for route in range(2):
                for d, i in enumerate(places):
                    block = jnp.stack([half[route, :, d] for half in halves], axis=1)
                    terms[route, i, :, :, start : start + 256] = block.reshape(N, 8, 256).astype(jnp.bfloat16)
        for i in reversed(places):
            for route in range(2):
                if i:
                    reduced[route][i] = send(
                        terms.at[route, i],
                        back.at[route, i],
                        r1s.at[route, i],
                        r1r.at[route, i],
                        along(route == 0, STEPS[i]),
                    )

    pairs = multiply(0)
    across = [cross(0, pairs)]
    pairs = multiply(1)
    across.append(cross(1, pairs))
    spread = [activate(g, across[g]) for g in range(2)]
    lower(0, forward(0, spread[0]))
    lower(1, forward(1, spread[1]))

    final = [[], []]
    for route in range(2):
        added = terms[route, 0].astype(jnp.float32)
        for i in range(1, N):
            reduced[route][i].wait_recv()
            added = added + back[route, i].astype(jnp.float32)
        onward[route] = added.astype(jnp.bfloat16)
        for i in (7, 5, 6, 3, 4, 1, 2):
            final[route].append(
                send(
                    onward.at[route, i],
                    last.at[route, i],
                    r2s.at[route, i],
                    r2r.at[route, i],
                    along(route == 1, STEPS[i]),
                )
            )
    sums = []
    for route in range(2):
        for copy in final[route]:
            copy.wait_recv()
        added = onward[route, 0].astype(jnp.float32)
        for i in range(1, N):
            added = added + last[route, i].astype(jnp.float32)
        sums.append(added)
    live = lax.broadcasted_iota(jnp.int32, (8, HALF), 0) < counts_ref[0]
    for half, part in enumerate(exchange(*sums)):
        lanes = slice(half * HALF, (half + 1) * HALF)
        out_ref[:, lanes] = jnp.where(live, hidden_ref[:, lanes] + part, 0.0).astype(jnp.bfloat16)
    for copy in sent:
        copy.wait_send()


def whole_layer(*operands):
    bf, f32 = jnp.bfloat16, jnp.float32
    dma = pltpu.SemaphoreType.DMA
    vmem = pltpu.VMEM
    return pl.pallas_call(
        kernel,
        out_shape=jax.ShapeDtypeStruct((8, 1024), bf),
        in_specs=[pl.BlockSpec(memory_space=pltpu.HBM)] * 12,
        out_specs=pl.BlockSpec(memory_space=vmem),
        scratch_shapes=[
            vmem((8, 1024), bf),
            vmem((8, 1024), bf),
            vmem((8, 512, 128), bf),
            vmem((8, 512, 128), bf),
            vmem((8, 128), bf),
            vmem((8, 128), bf),
            pltpu.SMEM((8,), jnp.int32),
            pltpu.SMEM((1,), jnp.int32),
            vmem((1024,), bf),
            vmem((64, 128), f32),
            vmem((8, 1024), f32),
            vmem((896, 1024), bf),
            vmem((UNITS, 1024), bf),
            vmem((2, N, N, 8, HALF), bf),
            vmem((2, N, N, 8, HALF), bf),
            vmem((2, N, N, 8, HALF), bf),
            vmem((2, N, 8, HALF), bf),
            vmem((2, N, 8, HALF), bf),
            dma((9,)),
            dma((4,)),
        ]
        + [dma((2, N))] * 8
        + [
            shape
            for count in [len(places) for places in GROUPS]
            for shape in (
                vmem((N, count, 8, 1024), bf),
                vmem((N, 1, 128), f32),
                vmem((4, count, 8, 896), bf),
                vmem((4, count, 8, 896), bf),
                vmem((4, 1, 128), f32),
                vmem((4, count, 8, 896), f32),
                vmem((NX, count, 8, 896), bf),
                vmem((NX, count, 8, 896), bf),
                vmem((NX, 1, 128), f32),
                vmem((NX, 1, 128), f32),
                vmem((2 * NX, count, 8, UNITS), bf),
                dma((2,)),
                dma((2,)),
                dma((2, NX)),
                dma((2, NX)),
                dma((NX,)),
                dma((NX,)),
                dma((NX,)),
                dma((NX,)),
            )
        ],
        compiler_params=pltpu.CompilerParams(
            collective_id=0, has_side_effects=True, vmem_limit_bytes=60 * 1024 * 1024
        ),
        cost_estimate=pl.CostEstimate(flops=1_430_000_000, bytes_accessed=5_000_000, transcendentals=0),
        name="whole_layer",
    )(*operands)


def on_device(
    residual,
    queries,
    cache_keys,
    cache_values,
    new_keys,
    new_values,
    lengths,
    counts,
    norm_gain,
    gate_weight,
    up_weight,
    down_weight,
):
    return whole_layer(
        residual,
        queries,
        cache_keys.reshape(8, 512, 128),
        cache_values.reshape(8, 512, 128),
        new_keys.reshape(8, 128),
        new_values.reshape(8, 128),
        lengths,
        counts,
        norm_gain,
        gate_weight,
        up_weight,
        down_weight,
    )


def solution(mesh):
    return jax.shard_map(
        on_device,
        mesh=mesh,
        in_specs=(
            P("attn", "ffn"),
            P("attn", "ffn"),
            P("attn", "ffn", None, None),
            P("attn", "ffn", None, None),
            P("attn", "ffn", None),
            P("attn", "ffn", None),
            P("attn"),
            P("attn"),
            P(),
            P("attn", "ffn"),
            P("attn", "ffn"),
            P("attn", "ffn"),
        ),
        out_specs=P("attn", "ffn"),
        check_vma=False,
    )
```

time: 71.5 us -> 64.6 us (0.903)
  Pallas kernels: 68.6 us -> 62.3 us
    pallas_call x1, Pallas kernels: 68.6 us -> 62.3 us  [whole_layer(): pl.pallas_call(kernel, out_shape=jax.ShapeDtypeStruct((8, 1024), bf), in_...]
where the time goes in v4:
time: 64.6 us; the launch traced here: 64.3 us
  Pallas kernels  62.3 us (96%)
  local copies, waits for them, and re-layouts  1.32 us (2%)
  between operations  0.66 us (1%)
    pallas_call x1, Pallas kernels, whole_layer(): pl.pallas_call(kernel, out_shape=jax.ShapeDtypeStruct((8, 1024), bf), in_...  62.3 us
    unnamed x1, local copies, waits for them, and re-layouts  1.32 us

profile of v4, /device:TPU:1, one launch (start us, length us, event | category | flops | bytes accessed | tf_op | source)
XLA Modules:
  0.0 64.3 jit_solution(16864666423583610623)
XLA Ops:
  0.7 62.3 %whole_layer.1 = bf16[8,1024]{1,0:T(8,128)(2,1)} custom-call(bf16[8,1024]{1,0:T(8,128)(2,1)} %residual_hbm.1, bf16[8,1024]{1,0:T(8,128)(2,1)} %queries_hbm.1, bf16[8,512,128]{2,1,0:T(8,128)(2,1)} %bitcast.4, bf16[8,512,128]{2,1,0:T(8,128)(2,1)} %bitcast.5, bf16[8,128]{1,0:T(8,128)(2,1)} %bitcast.6, bf16[8,128]{1,0:T(8,128)(2,1)} %bitcast.7, s32[8]{0:T(128)} %lengths_hbm.1, ...), custom_call_target="tpu_custom_call" | custom-call | flops 1430000000 | bytes 5000000 | tf_op jit(solution)/shard_map/whole_layer/pallas_call | solution.py:404
  63.0 1.3 %copy.15 = bf16[8,1024]{1,0:T(8,128)(2,1)} copy(bf16[8,1024]{1,0:T(8,128)(2,1)} %whole_layer.1) | data formatting | bytes 32768

commit v5 on v4

--- a/solution.py
+++ b/solution.py
@@ -205,37 +205,45 @@
         return at(z, lax.rem(y + (N + step), N), x, c)
 
     blocks = exchange(hidden_ref[:, :HALF], hidden_ref[:, HALF:])
-    first, second = [[], []], [{}, {}]
+    first, second = [{}, {}], [{}, {}]
     for route in range(2):
         held[route, 0, 0] = blocks[route].astype(jnp.bfloat16)
     for i in (7, 5, 6, 3, 4, 1, 2):
         for route in range(2):
-            first[route].append(
-                send(
-                    held.at[route, 0, 0],
-                    held.at[route, 0, i],
-                    g1s.at[route, i],
-                    g1r.at[route, i],
-                    along(route == 1, -STEPS[i]),
-                )
+            first[route][i] = send(
+                held.at[route, 0, 0],
+                held.at[route, 0, i],
+                g1s.at[route, i],
+                g1r.at[route, i],
+                along(route == 1, -STEPS[i]),
             )
 
-    def pass_on(route, i, source, device):
-        second[route][i] = send(
-            held.at[route, source], held.at[route, i], g2s.at[route, i], g2r.at[route, i], device
+    def pass_on(route, i, source, device, part):
+        span = (pl.ds(0, 5), pl.ds(5, 3), slice(None))[part]
+        second[route][i, part] = send(
+            held.at[route, source, span],
+            held.at[route, i, span],
+            g2s.at[route, part % 2, i],
+            g2r.at[route, part % 2, i],
+            device,
         )
 
+    for part, arrived in enumerate(((1, 2, 3, 4), (5, 6, 7))):
+        for route in range(2):
+            for i in arrived:
+                first[route][i].wait_recv()
+            for i in (3, 4):
+                pass_on(route, i, 0, along(route == 0, -STEPS[i]), part)
     for route in range(2):
-        for copy in first[route]:
-            copy.wait_recv()
-        for i in (3, 4, 1, 2):
-            pass_on(route, i, 0, along(route == 0, -STEPS[i]))
-    for route in range(2):
-        second[route][3].wait_recv()
-        second[route][4].wait_recv()
-        pass_on(route, 7, 3 + c, along(route == 0, -2 + 4 * c))
-        pass_on(route, 5, 3, along(route == 0, -1))
-        pass_on(route, 6, 4, along(route == 0, 1))
+        for i in (1, 2):
+            pass_on(route, i, 0, along(route == 0, -STEPS[i]), 2)
+    for part in range(2):
+        for route in range(2):
+            second[route][3, part].wait_recv()
+            second[route][4, part].wait_recv()
+            pass_on(route, 7, 3 + c, along(route == 0, -2 + 4 * c), part)
+            pass_on(route, 5, 3, along(route == 0, -1), part)
+            pass_on(route, 6, 4, along(route == 0, 1), part)
 
     def multiply(g):
         xs, ssb, pair_out, pair_in, pair_ss, own = by_group[g][:6]
@@ -246,8 +254,8 @@
         for route in range(2):
             squares = jnp.zeros((4, 1, 128), jnp.float32)
             for d, i in enumerate(places):
-                if i in (1, 2, 5, 6, 7):
-                    second[route][i].wait_recv()
+                for part in {1: (2,), 2: (2,), 5: (0, 1), 6: (0, 1), 7: (0, 1)}.get(i, ()):
+                    second[route][i, part].wait_recv()
                 packed = held[route, i].astype(jnp.float32).reshape(4, 2, 8, HALF)
                 low, high = exchange(packed[:, 0], packed[:, 1])
                 square = jnp.sum(low * low + high * high, axis=2, keepdims=True)
@@ -345,29 +353,42 @@
                 for d, i in enumerate(places):
                     block = jnp.stack([half[route, :, d] for half in halves], axis=1)
                     terms[route, i, :, :, start : start + 256] = block.reshape(N, 8, 256).astype(jnp.bfloat16)
-        for i in reversed(places):
+        for i in (1, 2) if g == 0 else (7, 5, 6):
             for route in range(2):
-                if i:
-                    reduced[route][i] = send(
-                        terms.at[route, i],
-                        back.at[route, i],
-                        r1s.at[route, i],
-                        r1r.at[route, i],
-                        along(route == 0, STEPS[i]),
-                    )
+                step = {1: 1, 2: -1, 5: 1, 6: -1, 7: 2 - 4 * c}[i]
+                add_up(route, i, along(route == 0, step))
+
+    def add_up(route, i, device):
+        reduced[route][i] = send(
+            terms.at[route, i], back.at[route, i], r1s.at[route, i], r1r.at[route, i], device
+        )
+
+    def relay(route):
+        for i in (5, 6, 7):
+            reduced[route][i].wait_recv()
+        straight, cut = terms[route, 3 + c].astype(jnp.float32), terms[route, 4 - c].astype(jnp.float32)
+        straight = straight + back[route, 5 + c].astype(jnp.float32) + back[route, 7].astype(jnp.float32)
+        cut = cut + back[route, 6 - c].astype(jnp.float32)
+        terms[route, 3 + c] = straight.astype(jnp.bfloat16)
+        terms[route, 4 - c] = cut.astype(jnp.bfloat16)
+        for i in (3, 4):
+            add_up(route, i, along(route == 0, STEPS[i]))
 
     pairs = multiply(0)
     across = [cross(0, pairs)]
     pairs = multiply(1)
     across.append(cross(1, pairs))
     spread = [activate(g, across[g]) for g in range(2)]
-    lower(0, forward(0, spread[0]))
-    lower(1, forward(1, spread[1]))
+    passed = [forward(g, spread[g]) for g in range(2)]
+    for g in range(2):
+        lower(g, passed[g])
+    for route in range(2):
+        relay(route)
 
     final = [[], []]
     for route in range(2):
         added = terms[route, 0].astype(jnp.float32)
-        for i in range(1, N):
+        for i in range(1, 5):
             reduced[route][i].wait_recv()
             added = added + back[route, i].astype(jnp.float32)
         onward[route] = added.astype(jnp.bfloat16)
@@ -428,7 +449,9 @@
             dma((9,)),
             dma((4,)),
         ]
-        + [dma((2, N))] * 8
+        + [dma((2, N))] * 2
+        + [dma((2, 2, N))] * 2
+        + [dma((2, N))] * 4
         + [
             shape
             for count in [len(places) for places in GROUPS]

time: 64.6 us -> 62.2 us (0.963)
  Pallas kernels: 62.3 us -> 59.9 us
    pallas_call x1, Pallas kernels: 62.3 us -> 59.9 us  [whole_layer(): pl.pallas_call(kernel, out_shape=jax.ShapeDtypeStruct((8, 1024), bf), in_...]
where the time goes in v5:
time: 62.2 us; the launch traced here: 61.9 us
  Pallas kernels  59.9 us (96%)
  local copies, waits for them, and re-layouts  1.32 us (2%)
  between operations  0.66 us (1%)
    pallas_call x1, Pallas kernels, whole_layer(): pl.pallas_call(kernel, out_shape=jax.ShapeDtypeStruct((8, 1024), bf), in_...  59.9 us
    unnamed x1, local copies, waits for them, and re-layouts  1.32 us

profile of v5, /device:TPU:1, one launch (start us, length us, event | category | flops | bytes accessed | tf_op | source)
XLA Modules:
  0.0 61.9 jit_solution(5862882842222433689)
XLA Ops:
  0.7 59.9 %whole_layer.1 = bf16[8,1024]{1,0:T(8,128)(2,1)} custom-call(bf16[8,1024]{1,0:T(8,128)(2,1)} %residual_hbm.1, bf16[8,1024]{1,0:T(8,128)(2,1)} %queries_hbm.1, bf16[8,512,128]{2,1,0:T(8,128)(2,1)} %bitcast.4, bf16[8,512,128]{2,1,0:T(8,128)(2,1)} %bitcast.5, bf16[8,128]{1,0:T(8,128)(2,1)} %bitcast.6, bf16[8,128]{1,0:T(8,128)(2,1)} %bitcast.7, s32[8]{0:T(128)} %lengths_hbm.1, ...), custom_call_target="tpu_custom_call" | custom-call | flops 1430000000 | bytes 5000000 | tf_op jit(solution)/shard_map/whole_layer/pallas_call | solution.py:425
  60.6 1.3 %copy.15 = bf16[8,1024]{1,0:T(8,128)(2,1)} copy(bf16[8,1024]{1,0:T(8,128)(2,1)} %whole_layer.1) | data formatting | bytes 32768

commit v6 on v5

--- a/solution.py
+++ b/solution.py
@@ -19,6 +19,7 @@
 MAIN = 384
 TILES = ((0, 256), (256, 256), (512, 256), (768, 128))
 STEPS = (0, 1, -1, 2, -2, 3, -3, 4)
+SPANS = (slice(0, 5), slice(5, 8), slice(0, 8))
 GROUPS = ((0, 1, 2, 3, 4), (5, 6, 7))
 
 
@@ -88,7 +89,6 @@
     new_keys_hbm,
     new_values_hbm,
     lengths_hbm,
-    counts_hbm,
     gain_hbm,
     gate_hbm,
     up_hbm,
@@ -101,7 +101,6 @@
     new_keys_ref,
     new_values_ref,
     lengths_ref,
-    counts_ref,
     gain_ref,
     by_head,
     hidden_ref,
@@ -148,7 +147,6 @@
                 (values_hbm, values_ref),
                 (new_values_hbm, new_values_ref),
                 (residual_hbm, residual_ref),
-                (counts_hbm, counts_ref),
                 (gain_hbm.at[pl.ds(ffn * 1024, 1024)], gain_ref),
             )
         )
@@ -219,7 +217,7 @@
             )
 
     def pass_on(route, i, source, device, part):
-        span = (pl.ds(0, 5), pl.ds(5, 3), slice(None))[part]
+        span = SPANS[part]
         second[route][i, part] = send(
             held.at[route, source, span],
             held.at[route, i, span],
@@ -353,26 +351,32 @@
                 for d, i in enumerate(places):
                     block = jnp.stack([half[route, :, d] for half in halves], axis=1)
                     terms[route, i, :, :, start : start + 256] = block.reshape(N, 8, 256).astype(jnp.bfloat16)
-        for i in (1, 2) if g == 0 else (7, 5, 6):
-            for route in range(2):
-                step = {1: 1, 2: -1, 5: 1, 6: -1, 7: 2 - 4 * c}[i]
-                add_up(route, i, along(route == 0, step))
-
-    def add_up(route, i, device):
-        reduced[route][i] = send(
-            terms.at[route, i], back.at[route, i], r1s.at[route, i], r1r.at[route, i], device
+        for part in (2,) if g == 0 else (1, 0):
+            for i in (1, 2) if g == 0 else (7, 5, 6):
+                for route in range(2):
+                    step = {1: 1, 2: -1, 5: 1, 6: -1, 7: 2 - 4 * c}[i]
+                    add_up(route, i, along(route == 0, step), part)
+
+    def add_up(route, i, device, part):
+        reduced[route][i, part] = send(
+            terms.at[route, i, SPANS[part]],
+            back.at[route, i, SPANS[part]],
+            r1s.at[part % 2, route, i],
+            r1r.at[part % 2, route, i],
+            device,
         )
 
-    def relay(route):
+    def relay(route, part):
         for i in (5, 6, 7):
-            reduced[route][i].wait_recv()
-        straight, cut = terms[route, 3 + c].astype(jnp.float32), terms[route, 4 - c].astype(jnp.float32)
-        straight = straight + back[route, 5 + c].astype(jnp.float32) + back[route, 7].astype(jnp.float32)
-        cut = cut + back[route, 6 - c].astype(jnp.float32)
-        terms[route, 3 + c] = straight.astype(jnp.bfloat16)
-        terms[route, 4 - c] = cut.astype(jnp.bfloat16)
+            reduced[route][i, part].wait_recv()
+        span = SPANS[part]
+        straight, cut = terms[route, 3 + c, span].astype(jnp.float32), terms[route, 4 - c, span].astype(jnp.float32)
+        straight = straight + back[route, 5 + c, span].astype(jnp.float32) + back[route, 7, span].astype(jnp.float32)
+        cut = cut + back[route, 6 - c, span].astype(jnp.float32)
+        terms[route, 3 + c, span] = straight.astype(jnp.bfloat16)
+        terms[route, 4 - c, span] = cut.astype(jnp.bfloat16)
         for i in (3, 4):
-            add_up(route, i, along(route == 0, STEPS[i]))
+            add_up(route, i, along(route == 0, STEPS[i]), part)
 
     pairs = multiply(0)
     across = [cross(0, pairs)]
@@ -382,26 +386,33 @@
     passed = [forward(g, spread[g]) for g in range(2)]
     for g in range(2):
         lower(g, passed[g])
-    for route in range(2):
-        relay(route)
+    for part in (1, 0):
+        for route in range(2):
+            relay(route, part)
 
     final = [[], []]
-    for route in range(2):
-        added = terms[route, 0].astype(jnp.float32)
-        for i in range(1, 5):
-            reduced[route][i].wait_recv()
-            added = added + back[route, i].astype(jnp.float32)
-        onward[route] = added.astype(jnp.bfloat16)
-        for i in (7, 5, 6, 3, 4, 1, 2):
-            final[route].append(
-                send(
-                    onward.at[route, i],
-                    last.at[route, i],
-                    r2s.at[route, i],
-                    r2r.at[route, i],
-                    along(route == 1, STEPS[i]),
+    for part in (1, 0):
+        span = SPANS[part]
+        for route in range(2):
+            if part:
+                for i in (1, 2):
+                    reduced[route][i, 2].wait_recv()
+            for i in (3, 4):
+                reduced[route][i, part].wait_recv()
+            added = terms[route, 0, span].astype(jnp.float32)
+            for i in range(1, 5):
+                added = added + back[route, i, span].astype(jnp.float32)
+            onward[route, span] = added.astype(jnp.bfloat16)
+            for i in ((3, 4, 1, 2), (7, 5, 6))[part]:
+                final[route].append(
+                    send(
+                        onward.at[route, i],
+                        last.at[route, i],
+                        r2s.at[route, i],
+                        r2r.at[route, i],
+                        along(route == 1, STEPS[i]),
+                    )
                 )
-            )
     sums = []
     for route in range(2):
         for copy in final[route]:
@@ -410,10 +421,9 @@
         for i in range(1, N):
             added = added + last[route, i].astype(jnp.float32)
         sums.append(added)
-    live = lax.broadcasted_iota(jnp.int32, (8, HALF), 0) < counts_ref[0]
     for half, part in enumerate(exchange(*sums)):
         lanes = slice(half * HALF, (half + 1) * HALF)
-        out_ref[:, lanes] = jnp.where(live, hidden_ref[:, lanes] + part, 0.0).astype(jnp.bfloat16)
+        out_ref[:, lanes] = (hidden_ref[:, lanes] + part).astype(jnp.bfloat16)
     for copy in sent:
         copy.wait_send()
 
@@ -425,7 +435,7 @@
     return pl.pallas_call(
         kernel,
         out_shape=jax.ShapeDtypeStruct((8, 1024), bf),
-        in_specs=[pl.BlockSpec(memory_space=pltpu.HBM)] * 12,
+        in_specs=[pl.BlockSpec(memory_space=pltpu.HBM)] * 11,
         out_specs=pl.BlockSpec(memory_space=vmem),
         scratch_shapes=[
             vmem((8, 1024), bf),
@@ -435,7 +445,6 @@
             vmem((8, 128), bf),
             vmem((8, 128), bf),
             pltpu.SMEM((8,), jnp.int32),
-            pltpu.SMEM((1,), jnp.int32),
             vmem((1024,), bf),
             vmem((64, 128), f32),
             vmem((8, 1024), f32),
@@ -446,12 +455,12 @@
             vmem((2, N, N, 8, HALF), bf),
             vmem((2, N, 8, HALF), bf),
             vmem((2, N, 8, HALF), bf),
-            dma((9,)),
+            dma((8,)),
             dma((4,)),
         ]
         + [dma((2, N))] * 2
-        + [dma((2, 2, N))] * 2
-        + [dma((2, N))] * 4
+        + [dma((2, 2, N))] * 4
+        + [dma((2, N))] * 2
         + [
             shape
             for count in [len(places) for places in GROUPS]
@@ -499,7 +508,7 @@
     up_weight,
     down_weight,
 ):
-    return whole_layer(
+    result = whole_layer(
         residual,
         queries,
         cache_keys.reshape(8, 512, 128),
@@ -507,12 +516,13 @@
         new_keys.reshape(8, 128),
         new_values.reshape(8, 128),
         lengths,
-        counts,
         norm_gain,
         gate_weight,
         up_weight,
         down_weight,
     )
+    is_live = jnp.arange(8, dtype=jnp.int32) < counts[0]
+    return jnp.where(is_live[:, None], result, jnp.zeros_like(result))
 
 
 def solution(mesh):

time: 62.2 us -> 61.4 us (0.987)
  other arithmetic: 0 us -> 1.4 us
  local copies, waits for them, and re-layouts: 1.32 us -> 0 us
  Pallas kernels: 59.9 us -> 59.1 us
    select_n x0 -> x1, other arithmetic: none -> 1.4 us  [on_device(): return jnp.where(is_live[:, None], result, jnp.zeros_like(result))]
    unnamed x1 -> x0, local copies, waits for them, and re-layouts: 1.32 us -> none
    pallas_call x1, Pallas kernels: 59.9 us -> 59.1 us  [whole_layer(): pl.pallas_call(kernel, out_shape=jax.ShapeDtypeStruct((8, 1024), bf), in_...]
where the time goes in v6:
time: 61.4 us; the launch traced here: 61.1 us
  Pallas kernels  59.1 us (96%)
  other arithmetic  1.4 us (2%)
  between operations  0.67 us (1%)
    pallas_call x1, Pallas kernels, whole_layer(): pl.pallas_call(kernel, out_shape=jax.ShapeDtypeStruct((8, 1024), bf), in_...  59.1 us
    select_n x1, other arithmetic, on_device(): return jnp.where(is_live[:, None], result, jnp.zeros_like(result))  1.4 us

profile of v6, /device:TPU:1, one launch (start us, length us, event | category | flops | bytes accessed | tf_op | source)
XLA Modules:
  0.0 61.1 jit_solution(6970639983818199626)
XLA Ops:
  0.7 59.1 %whole_layer.1 = bf16[8,1024]{1,0:T(8,128)(2,1)} custom-call(bf16[8,1024]{1,0:T(8,128)(2,1)} %residual_hbm.1, bf16[8,1024]{1,0:T(8,128)(2,1)} %queries_hbm.1, bf16[8,512,128]{2,1,0:T(8,128)(2,1)} %bitcast.6, bf16[8,512,128]{2,1,0:T(8,128)(2,1)} %bitcast.7, bf16[8,128]{1,0:T(8,128)(2,1)} %bitcast.8, bf16[8,128]{1,0:T(8,128)(2,1)} %bitcast.9, s32[8]{0:T(128)} %lengths_hbm.1, ...), custom_call_target="tpu_custom_call" | custom-call | flops 1430000000 | bytes 5000000 | tf_op jit(solution)/shard_map/whole_layer/pallas_call | solution.py:435
  59.7 1.4 %broadcast_select_fusion = bf16[8,1024]{1,0:T(8,128)(2,1)} fusion(bf16[8,1024]{1,0:T(8,128)(2,1)} %whole_layer.1, pred[8]{0:T(512)(128)(4,1)S(1)} %iota_compare_fusion), kind=kLoop, calls=%fused_computation | loop fusion | flops 8192 | bytes 32776 | tf_op jit(solution)/shard_map/jit(_where)/select_n | solution.py:525
  (1 shorter events, 0.0 us)

commit v7 on v6

v7 whole, which is shorter than its diff:
```python
import jax
import jax.numpy as jnp
from jax import lax
from jax.experimental import pallas as pl
from jax.experimental.pallas import tpu as pltpu
from jax.sharding import PartitionSpec as P

D = 8192


epsilon = 1e-05


MESH = pl.DeviceIdType.MESH
N = 8
NX = 4
WIDE = 1024
UNITS = 448
MAIN = 384
TILES = ((0, 256), (256, 256), (512, 256), (768, 128))
STEPS = (0, 1, -1, 2, -2, 3, -3, 4)
SPANS = (slice(0, 5), slice(5, 8), slice(0, 8))
GROUPS = ((0, 1, 2, 3, 4), (5, 6, 7))


def transposed_dot(rows, weight):
    return lax.dot_general(rows, weight, (((1,), (1,)), ((), ())), preferred_element_type=jnp.float32)


def exchange(low, high):
    axis = low.ndim - 2
    upper = lax.broadcasted_iota(jnp.int32, low.shape, axis) < 4
    return jnp.where(upper, low, pltpu.roll(high, 4, axis)), jnp.where(upper, pltpu.roll(low, 4, axis), high)


def attend(
    inputs,
    queries_ref,
    keys_ref,
    values_ref,
    new_keys_ref,
    new_values_ref,
    lengths_ref,
    residual_ref,
    by_head,
    hidden_ref,
):
    for load in inputs[:4]:
        load.wait()
    score_scale = 1.0 / 128**0.5
    for h in range(8):
        by_head[h * 8 : h * 8 + 8, :] = queries_ref[:, h * 128 : h * 128 + 128].astype(jnp.float32)
    new_keys = new_keys_ref[...].astype(jnp.float32)
    position = lax.broadcasted_iota(jnp.int32, (8, 512), 1)
    scores = []
    own = []
    for r in range(8):
        query = by_head[pl.ds(r, 8, stride=8), :]
        own.append(jnp.sum(query * new_keys[r : r + 1, :], axis=1, keepdims=True))
        slot = transposed_dot(query.astype(jnp.bfloat16), keys_ref[r]) * score_scale
        scores.append(jnp.where(position < lengths_ref[r], slot, -1e30))
    scores = jnp.concatenate(scores, axis=0)
    own = jnp.concatenate(own, axis=0) * score_scale
    row_max = jnp.maximum(jnp.max(scores, axis=1, keepdims=True), own)
    key_weights = jnp.exp(scores - row_max)
    own_weight = jnp.exp(own - row_max)
    denominator = jnp.sum(key_weights, axis=1, keepdims=True) + own_weight
    key_probs = key_weights / denominator
    own_prob = (own_weight / denominator).astype(jnp.bfloat16).astype(jnp.float32)
    for load in inputs[4:]:
        load.wait()
    new_values = new_values_ref[...].astype(jnp.float32)
    for r in range(8):
        probs = key_probs[r * 8 : r * 8 + 8, :].astype(jnp.bfloat16)
        mixed = jnp.dot(probs, values_ref[r], preferred_element_type=jnp.float32)
        mixed = mixed + own_prob[r * 8 : r * 8 + 8, :] * new_values[r : r + 1, :]
        by_head[pl.ds(r, 8, stride=8), :] = mixed.astype(jnp.bfloat16).astype(jnp.float32)
    for h in range(8):
        lanes = slice(h * 128, h * 128 + 128)
        hidden = residual_ref[:, lanes].astype(jnp.float32) + by_head[h * 8 : h * 8 + 8, :]
        hidden_ref[:, lanes] = hidden.astype(jnp.bfloat16).astype(jnp.float32)


def kernel(
    residual_hbm,
    queries_hbm,
    keys_hbm,
    values_hbm,
    new_keys_hbm,
    new_values_hbm,
    lengths_hbm,
    gain_hbm,
    gate_hbm,
    up_hbm,
    down_hbm,
    out_ref,
    residual_ref,
    queries_ref,
    keys_ref,
    values_ref,
    new_keys_ref,
    new_values_ref,
    lengths_ref,
    gain_ref,
    by_head,
    hidden_ref,
    gu,
    down,
    swap,
    held,
    terms,
    back,
    onward,
    last,
    result,
    asem,
    wsem,
    sws,
    swr,
    g1s,
    g1r,
    g2s,
    g2r,
    r1s,
    r1r,
    r2s,
    r2r,
    *by_group,
):
    each = len(by_group) // len(GROUPS)
    by_group = [by_group[g * each : g * each + each] for g in range(len(GROUPS))]
    attn = lax.axis_index("attn")
    ffn = lax.axis_index("ffn")
    z, y = lax.div(attn, N), lax.rem(attn, N)
    x, c = lax.div(ffn, 2), lax.rem(ffn, 2)

    def at(zz, yy, xx, cc):
        return (zz * N + yy, xx * 2 + cc)

    def past(i, k, n):
        return lax.rem(i + k, n)

    inputs = [
        pltpu.make_async_copy(source, target, asem.at[i])
        for i, (source, target) in enumerate(
            (
                (queries_hbm, queries_ref),
                (new_keys_hbm, new_keys_ref),
                (lengths_hbm, lengths_ref),
                (keys_hbm, keys_ref),
                (values_hbm, values_ref),
                (new_values_hbm, new_values_ref),
                (residual_hbm, residual_ref),
                (gain_hbm.at[pl.ds(x * 2048, 2048)], gain_ref),
            )
        )
    ]
    for load in inputs:
        load.start()
    loads = [
        pltpu.make_async_copy(gate_hbm, gu.at[c, pl.ds(0, UNITS)], wsem.at[0]),
        pltpu.make_async_copy(up_hbm.at[pl.ds(MAIN, UNITS - MAIN)], gu.at[c, pl.ds(UNITS, UNITS - MAIN)], wsem.at[1]),
        pltpu.make_async_copy(up_hbm.at[pl.ds(0, MAIN)], gu.at[c, pl.ds(512, MAIN)], wsem.at[2]),
        pltpu.make_async_copy(down_hbm, down.at[c], wsem.at[3]),
    ]
    for load in loads:
        load.start()

    barrier = pltpu.get_barrier_semaphore()
    partners = [at(past(z, k, N), y, x, c) for k in range(1, N)]
    partners += [at(z, past(y, k, N), x, c) for k in range(1, N)]
    partners += [at(z, y, past(x, k, NX), c) for k in range(1, NX)]
    partners += [at(z, y, x, 1 - c)]
    for partner in partners:
        pl.semaphore_signal(barrier, inc=1, device_id=partner, device_id_type=MESH)

    attend(
        inputs,
        queries_ref,
        keys_ref,
        values_ref,
        new_keys_ref,
        new_values_ref,
        lengths_ref,
        residual_ref,
        by_head,
        hidden_ref,
    )
    gain = gain_ref[...].astype(jnp.float32).reshape(1, 2048)
    swap[c] = hidden_ref[...].astype(jnp.bfloat16)
    pl.semaphore_wait(barrier, len(partners))

    sent = []

    def send(source, target, send_sem, recv_sem, device):
        copy = pltpu.make_async_remote_copy(
            src_ref=source, dst_ref=target, send_sem=send_sem, recv_sem=recv_sem, device_id=device, device_id_type=MESH
        )
        copy.start()
        sent.append(copy)
        return copy

    other = at(z, y, x, 1 - c)

    def along(second_axis, step):
        on_z = 1 - c if second_axis else c
        return at(lax.rem(z + N + step * on_z, N), lax.rem(y + N + step * (1 - on_z), N), x, c)

    swapped = [send(swap.at[c], swap.at[c], sws.at[0], swr.at[0], other)]
    for load in loads:
        load.wait()
    swapped[0].wait_recv()

    blocks = exchange(swap[0].astype(jnp.float32), swap[1].astype(jnp.float32))
    held[0, 0] = jnp.where(c == 0, blocks[0], blocks[1]).astype(jnp.bfloat16)
    first, second = {}, {}
    for i in (7, 5, 6, 3, 4, 1, 2):
        first[i] = send(held.at[0, 0], held.at[0, i], g1s.at[i], g1r.at[i], along(False, -STEPS[i]))
    swapped.append(send(gu.at[c], gu.at[c], sws.at[1], swr.at[1], other))
    swapped.append(send(down.at[c], down.at[c], sws.at[2], swr.at[2], other))

    def pass_on(i, source, step, part):
        span = SPANS[part]
        second[i, part] = send(
            held.at[source, span],
            held.at[i, span],
            g2s.at[part % 2, i],
            g2r.at[part % 2, i],
            along(True, step),
        )

    for part, arrived in enumerate(((1, 2, 3, 4), (5, 6, 7))):
        for i in arrived:
            first[i].wait_recv()
        for i in (3, 4):
            pass_on(i, 0, -STEPS[i], part)
    for i in (1, 2):
        pass_on(i, 0, -STEPS[i], 2)
    for part in range(2):
        second[3, part].wait_recv()
        second[4, part].wait_recv()
        pass_on(7, 3 + part, -2 + 4 * part, part)
        pass_on(5, 3, -1, part)
        pass_on(6, 4, 1, part)

    def multiply(g):
        xs, ssb, own = by_group[g][:3]
        places = GROUPS[g]
        count = len(places)
        lane = lax.broadcasted_iota(jnp.int32, (4, 8, 128), 2)
        row = lax.broadcasted_iota(jnp.int32, (4, 8, 128), 1)
        squares = jnp.zeros((4, 1, 128), jnp.float32)
        for d, i in enumerate(places):
            for part in {1: (2,), 2: (2,), 5: (0, 1), 6: (0, 1), 7: (0, 1)}.get(i, ()):
                second[i, part].wait_recv()
            packed = held[i].astype(jnp.float32).reshape(4, 2, 8, WIDE)
            low, high = exchange(packed[:, 0], packed[:, 1])
            square = jnp.sum(low * low + high * high, axis=2, keepdims=True)
            squares = squares + jnp.sum(jnp.where(lane == row + 8 * d, square, 0.0), axis=1, keepdims=True)
            xs[0, :, d] = (low * gain[:, :WIDE]).astype(jnp.bfloat16)
            xs[1, :, d] = (high * gain[:, WIDE:]).astype(jnp.bfloat16)
        ssb[...] = squares
        if g == 0:
            swapped[1].wait_recv()
        rows = [xs[core].reshape(32 * count, WIDE) for core in range(2)]
        for start, width in TILES:
            block = transposed_dot(rows[0], gu[0, start : start + width, :])
            block = block + transposed_dot(rows[1], gu[1, start : start + width, :])
            own[:, :, :, start : start + width] = block.reshape(4, count, 8, width)

    def cross(g):
        ssb, own, x_out, x_in, x_ss_out, x_ss_in = by_group[g][1:7]
        xss, xsr = by_group[g][8:10]
        copies = []
        for k in (2, 1, 3):
            xx = past(x, k, NX)
            x_out[k] = own[xx].astype(jnp.bfloat16)
            x_ss_out[k] = ssb[xx]
            device = at(z, y, xx, c)
            copies.append(send(x_out.at[k], x_in.at[k], xss.at[0, k], xsr.at[0, k], device))
            copies.append(send(x_ss_out.at[k], x_ss_in.at[k], xss.at[1, k], xsr.at[1, k], device))
        return copies

    def activate(g, before):
        ssb, own, _, x_in, _, x_ss_in, act = by_group[g][1:8]
        acs, acr = by_group[g][10:12]
        count = len(GROUPS[g])
        total = own[x]
        squares = ssb[x]
        for copy in before:
            copy.wait_recv()
        for k in range(1, NX):
            total = total + x_in[k].astype(jnp.float32)
            squares = squares + x_ss_in[k]
        total = total.reshape(8 * count, 896)
        lane = lax.broadcasted_iota(jnp.int32, (8 * count, 128), 1)
        row = lax.broadcasted_iota(jnp.int32, (8 * count, 128), 0)
        mean_square = jnp.sum(jnp.where(lane == row, squares, 0.0), axis=1, keepdims=True) / D
        total = total * lax.rsqrt(mean_square + epsilon)
        gate = total[:, :512]
        silu = gate / (1.0 + jnp.exp(-gate))
        main = (silu[:, :MAIN] * total[:, 512:]).astype(jnp.bfloat16)
        act[x, :, :, :MAIN] = main.reshape(count, 8, MAIN)
        tail = (silu[:, MAIN:] * pltpu.roll(total[:, MAIN:512], 64, 1))[:, : UNITS - MAIN]
        act[x, :, :, MAIN:] = tail.astype(jnp.bfloat16).reshape(count, 8, UNITS - MAIN)
        copies = []
        for k in (2, 1, 3):
            device = at(z, y, past(x, k, NX), c)
            copies.append(send(act.at[x], act.at[x], acs.at[k], acr.at[k], device))
        return copies

    reduced = {}

    def lower(g, before):
        act = by_group[g][7]
        places = GROUPS[g]
        count = len(places)
        for copy in before:
            copy.wait_recv()
        if g == 0:
            swapped[2].wait_recv()
        rows = act[...].reshape(32 * count, UNITS)
        for start in range(0, WIDE, 256):
            quarters = [
                jnp.dot(rows, down[core, :, start : start + 256], preferred_element_type=jnp.float32)
                for core in range(2)
            ]
            halves = exchange(*[quarter.reshape(4, count, 8, 256) for quarter in quarters])
            for d, i in enumerate(places):
                block = jnp.stack([half[:, d] for half in halves], axis=1)
                terms[i, :, :, start : start + 256] = block.reshape(N, 8, 256).astype(jnp.bfloat16)
        for part in (2,) if g == 0 else (1, 0):
            for i in (1, 2) if g == 0 else (7, 5, 6):
                add_up(i, {1: 1, 2: -1, 5: 1, 6: -1, 7: 2 - 4 * part}[i], part)

    def add_up(i, step, part):
        reduced[i, part] = send(
            terms.at[i, SPANS[part]],
            back.at[i, SPANS[part]],
            r1s.at[part % 2, i],
            r1r.at[part % 2, i],
            along(True, step),
        )

    def relay(part):
        for i in (5, 6, 7):
            reduced[i, part].wait_recv()
        span = SPANS[part]
        straight, cut = terms[3 + part, span].astype(jnp.float32), terms[4 - part, span].astype(jnp.float32)
        straight = straight + back[5 + part, span].astype(jnp.float32) + back[7, span].astype(jnp.float32)
        cut = cut + back[6 - part, span].astype(jnp.float32)
        terms[3 + part, span] = straight.astype(jnp.bfloat16)
        terms[4 - part, span] = cut.astype(jnp.bfloat16)
        for i in (3, 4):
            add_up(i, STEPS[i], part)

    across = []
    for g in range(2):
        multiply(g)
        across.append(cross(g))
    spread = [activate(g, across[g]) for g in range(2)]
    for g in range(2):
        lower(g, spread[g])
    for part in (1, 0):
        relay(part)

    final = []
    for part in (1, 0):
        span = SPANS[part]
        if part:
            for i in (1, 2):
                reduced[i, 2].wait_recv()
        for i in (3, 4):
            reduced[i, part].wait_recv()
        added = terms[0, span].astype(jnp.float32)
        for i in range(1, 5):
            added = added + back[i, span].astype(jnp.float32)
        onward[span] = added.astype(jnp.bfloat16)
        for i in ((3, 4, 1, 2), (7, 5, 6))[part]:
            final.append(send(onward.at[i], last.at[i], r2s.at[i], r2r.at[i], along(False, STEPS[i])))
    for copy in final:
        copy.wait_recv()
    added = onward[0].astype(jnp.float32)
    for i in range(1, N):
        added = added + last[i].astype(jnp.float32)
    result[c] = added
    send(result.at[c], result.at[c], sws.at[3], swr.at[3], other).wait_recv()
    low, high = exchange(result[0], result[1])
    out_ref[...] = (hidden_ref[...] + jnp.where(c == 0, low, high)).astype(jnp.bfloat16)
    for copy in sent:
        copy.wait_send()


def whole_layer(*operands):
    bf, f32 = jnp.bfloat16, jnp.float32
    dma = pltpu.SemaphoreType.DMA
    vmem = pltpu.VMEM
    return pl.pallas_call(
        kernel,
        out_shape=jax.ShapeDtypeStruct((8, 1024), bf),
        in_specs=[pl.BlockSpec(memory_space=pltpu.HBM)] * 11,
        out_specs=pl.BlockSpec(memory_space=vmem),
        scratch_shapes=[
            vmem((8, 1024), bf),
            vmem((8, 1024), bf),
            vmem((8, 512, 128), bf),
            vmem((8, 512, 128), bf),
            vmem((8, 128), bf),
            vmem((8, 128), bf),
            pltpu.SMEM((8,), jnp.int32),
            vmem((2048,), bf),
            vmem((64, 128), f32),
            vmem((8, 1024), f32),
            vmem((2, 896, WIDE), bf),
            vmem((2, UNITS, WIDE), bf),
            vmem((2, 8, WIDE), bf),
            vmem((N, N, 8, WIDE), bf),
            vmem((N, N, 8, WIDE), bf),
            vmem((N, N, 8, WIDE), bf),
            vmem((N, 8, WIDE), bf),
            vmem((N, 8, WIDE), bf),
            vmem((2, 8, WIDE), f32),
            dma((8,)),
            dma((4,)),
            dma((4,)),
            dma((4,)),
        ]
        + [dma((N,))] * 2
        + [dma((2, N))] * 4
        + [dma((N,))] * 2
        + [
            shape
            for count in [len(places) for places in GROUPS]
            for shape in (
                vmem((2, 4, count, 8, WIDE), bf),
                vmem((4, 1, 128), f32),
                vmem((4, count, 8, 896), f32),
                vmem((NX, count, 8, 896), bf),
                vmem((NX, count, 8, 896), bf),
                vmem((NX, 1, 128), f32),
                vmem((NX, 1, 128), f32),
                vmem((NX, count, 8, UNITS), bf),
                dma((2, NX)),
                dma((2, NX)),
                dma((NX,)),
                dma((NX,)),
            )
        ],
        compiler_params=pltpu.CompilerParams(
            collective_id=0, has_side_effects=True, vmem_limit_bytes=60 * 1024 * 1024
        ),
        cost_estimate=pl.CostEstimate(flops=1_430_000_000, bytes_accessed=5_000_000, transcendentals=0),
        name="whole_layer",
    )(*operands)


def on_device(
    residual,
    queries,
    cache_keys,
    cache_values,
    new_keys,
    new_values,
    lengths,
    counts,
    norm_gain,
    gate_weight,
    up_weight,
    down_weight,
):
    result = whole_layer(
        residual,
        queries,
        cache_keys.reshape(8, 512, 128),
        cache_values.reshape(8, 512, 128),
        new_keys.reshape(8, 128),
        new_values.reshape(8, 128),
        lengths,
        norm_gain,
        gate_weight,
        up_weight,
        down_weight,
    )
    is_live = jnp.arange(8, dtype=jnp.int32) < counts[0]
    return jnp.where(is_live[:, None], result, jnp.zeros_like(result))


def solution(mesh):
    return jax.shard_map(
        on_device,
        mesh=mesh,
        in_specs=(
            P("attn", "ffn"),
            P("attn", "ffn"),
            P("attn", "ffn", None, None),
            P("attn", "ffn", None, None),
            P("attn", "ffn", None),
            P("attn", "ffn", None),
            P("attn"),
            P("attn"),
            P(),
            P("attn", "ffn"),
            P("attn", "ffn"),
            P("attn", "ffn"),
        ),
        out_specs=P("attn", "ffn"),
        check_vma=False,
    )
```

time: 61.4 us -> 63.1 us (1.028)
  Pallas kernels: 59.1 us -> 60.7 us
    pallas_call x1, Pallas kernels: 59.1 us -> 60.7 us  [whole_layer(): pl.pallas_call(kernel, out_shape=jax.ShapeDtypeStruct((8, 1024), bf), in_...]
where the time goes in v7:
time: 63.1 us; the launch traced here: 62.8 us
  Pallas kernels  60.7 us (96%)
  other arithmetic  1.4 us (2%)
  between operations  0.67 us (1%)
    pallas_call x1, Pallas kernels, whole_layer(): pl.pallas_call(kernel, out_shape=jax.ShapeDtypeStruct((8, 1024), bf), in_...  60.7 us
    select_n x1, other arithmetic, on_device(): return jnp.where(is_live[:, None], result, jnp.zeros_like(result))  1.4 us

profile of v7, /device:TPU:1, one launch (start us, length us, event | category | flops | bytes accessed | tf_op | source)
XLA Modules:
  0.0 62.8 jit_solution(3247159843432115403)
XLA Ops:
  0.7 60.7 %whole_layer.1 = bf16[8,1024]{1,0:T(8,128)(2,1)} custom-call(bf16[8,1024]{1,0:T(8,128)(2,1)} %residual_hbm.1, bf16[8,1024]{1,0:T(8,128)(2,1)} %queries_hbm.1, bf16[8,512,128]{2,1,0:T(8,128)(2,1)} %bitcast.6, bf16[8,512,128]{2,1,0:T(8,128)(2,1)} %bitcast.7, bf16[8,128]{1,0:T(8,128)(2,1)} %bitcast.8, bf16[8,128]{1,0:T(8,128)(2,1)} %bitcast.9, s32[8]{0:T(128)} %lengths_hbm.1, ...), custom_call_target="tpu_custom_call" | custom-call | flops 1430000000 | bytes 5000000 | tf_op jit(solution)/shard_map/whole_layer/pallas_call | solution.py:398
  61.4 1.4 %broadcast_select_fusion = bf16[8,1024]{1,0:T(8,128)(2,1)} fusion(bf16[8,1024]{1,0:T(8,128)(2,1)} %whole_layer.1, pred[8]{0:T(512)(128)(4,1)S(1)} %iota_compare_fusion), kind=kLoop, calls=%fused_computation | loop fusion | flops 8192 | bytes 32776 | tf_op jit(solution)/shard_map/jit(_where)/select_n | solution.py:485
  (1 shorter events, 0.0 us)

commit v8 on v6

--- a/solution.py
+++ b/solution.py
@@ -165,7 +165,7 @@
     barrier = pltpu.get_barrier_semaphore()
     partners = [at(past(z, k, N), y, x, c) for k in range(1, N)]
     partners += [at(z, past(y, k, N), x, c) for k in range(1, N)]
-    partners += [at(z, y, past(x, k, NX), c) for k in range(1, NX)]
+    partners += [at(z, y, past(x, k, NX), core) for k in range(1, NX) for core in (c, 1 - c)]
     partners += [at(z, y, x, 1 - c)]
     for partner in partners:
         pl.semaphore_signal(barrier, inc=1, device_id=partner, device_id_type=MESH)
@@ -320,12 +320,19 @@
         for k in (2, 1, 3):
             device = at(z, y, past(x, k, NX), c)
             copies.append(send(act.at[mine], act.at[mine], acs.at[k], acr.at[k], device))
-        return copies, [send(act.at[mine], act.at[mine], fws.at[0], fwr.at[0], other)]
+        passed = [send(act.at[mine], act.at[mine], fws.at[0], fwr.at[0], other)]
+        if g == 1:
+            for k in (2, 1, 3):
+                device = at(z, y, past(x, k, NX), 1 - c)
+                passed.append(send(act.at[mine], act.at[mine], fws.at[k], fwr.at[k], device))
+        return copies, passed
 
     def forward(g, before):
         act = by_group[g][10]
         fws, fwr = by_group[g][17:19]
         copies, passed = before
+        if g == 1:
+            return copies + passed
         for k, copy in zip((1, 3, 2), (copies[1], copies[2], copies[0])):
             copy.wait_recv()
             place = c * 4 + past(x, NX - k, NX)
@@ -390,6 +397,7 @@
         for route in range(2):
             relay(route, part)
 
+    early = len(sent)
     final = [[], []]
     for part in (1, 0):
         span = SPANS[part]
@@ -413,6 +421,8 @@
                         along(route == 1, STEPS[i]),
                     )
                 )
+    for copy in sent[:early]:
+        copy.wait_send()
     sums = []
     for route in range(2):
         for copy in final[route]:
@@ -424,7 +434,7 @@
     for half, part in enumerate(exchange(*sums)):
         lanes = slice(half * HALF, (half + 1) * HALF)
         out_ref[:, lanes] = (hidden_ref[:, lanes] + part).astype(jnp.bfloat16)
-    for copy in sent:
+    for copy in sent[early:]:
         copy.wait_send()
 
 

time: 61.4 us -> 60.7 us (0.989)
  Pallas kernels: 59.1 us -> 58.3 us
    pallas_call x1, Pallas kernels: 59.1 us -> 58.3 us  [whole_layer(): pl.pallas_call(kernel, out_shape=jax.ShapeDtypeStruct((8, 1024), bf), in_...]
where the time goes in v8:
time: 60.7 us; the launch traced here: 60.3 us
  Pallas kernels  58.3 us (96%)
  other arithmetic  1.4 us (2%)
  between operations  0.67 us (1%)
    pallas_call x1, Pallas kernels, whole_layer(): pl.pallas_call(kernel, out_shape=jax.ShapeDtypeStruct((8, 1024), bf), in_...  58.3 us
    select_n x1, other arithmetic, on_device(): return jnp.where(is_live[:, None], result, jnp.zeros_like(result))  1.4 us

profile of v8, /device:TPU:1, one launch (start us, length us, event | category | flops | bytes accessed | tf_op | source)
XLA Modules:
  0.0 60.3 jit_solution(15432793349468514299)
XLA Ops:
  0.7 58.3 %whole_layer.1 = bf16[8,1024]{1,0:T(8,128)(2,1)} custom-call(bf16[8,1024]{1,0:T(8,128)(2,1)} %residual_hbm.1, bf16[8,1024]{1,0:T(8,128)(2,1)} %queries_hbm.1, bf16[8,512,128]{2,1,0:T(8,128)(2,1)} %bitcast.6, bf16[8,512,128]{2,1,0:T(8,128)(2,1)} %bitcast.7, bf16[8,128]{1,0:T(8,128)(2,1)} %bitcast.8, bf16[8,128]{1,0:T(8,128)(2,1)} %bitcast.9, s32[8]{0:T(128)} %lengths_hbm.1, ...), custom_call_target="tpu_custom_call" | custom-call | flops 1430000000 | bytes 5000000 | tf_op jit(solution)/shard_map/whole_layer/pallas_call | solution.py:445
  58.9 1.4 %broadcast_select_fusion = bf16[8,1024]{1,0:T(8,128)(2,1)} fusion(bf16[8,1024]{1,0:T(8,128)(2,1)} %whole_layer.1, pred[8]{0:T(512)(128)(4,1)S(1)} %iota_compare_fusion), kind=kLoop, calls=%fused_computation | loop fusion | flops 8192 | bytes 32776 | tf_op jit(solution)/shard_map/jit(_where)/select_n | solution.py:535
  (1 shorter events, 0.0 us)

commit v9 on v8

--- a/solution.py
+++ b/solution.py
@@ -497,7 +497,7 @@
             )
         ],
         compiler_params=pltpu.CompilerParams(
-            collective_id=0, has_side_effects=True, vmem_limit_bytes=60 * 1024 * 1024
+            collective_id=0, has_side_effects=True, vmem_limit_bytes=(53 * 1024 + 924) * 1024
         ),
         cost_estimate=pl.CostEstimate(flops=1_430_000_000, bytes_accessed=5_000_000, transcendentals=0),
         name="whole_layer",

time: 60.7 us -> 59.7 us (0.984)
  Pallas kernels: 58.3 us -> 57.5 us
  other arithmetic: 1.4 us -> 0.69 us
  local copies, waits for them, and re-layouts: 0 us -> 0.68 us
    pallas_call x1, Pallas kernels: 58.3 us -> 57.5 us  [whole_layer(): pl.pallas_call(kernel, out_shape=jax.ShapeDtypeStruct((8, 1024), bf), in_...]
    select_n x1, other arithmetic: 1.4 us -> 0.68 us  [on_device(): return jnp.where(is_live[:, None], result, jnp.zeros_like(result))]
    unnamed x0 -> x6, local copies, waits for them, and re-layouts: none -> 0.68 us
where the time goes in v9:
time: 59.7 us; the launch traced here: 59.5 us
  Pallas kernels  57.5 us (96%)
  other arithmetic  0.69 us (1%)
  between operations  0.69 us (1%)
  local copies, waits for them, and re-layouts  0.68 us (1%)
    pallas_call x1, Pallas kernels, whole_layer(): pl.pallas_call(kernel, out_shape=jax.ShapeDtypeStruct((8, 1024), bf), in_...  57.5 us

profile of v9, /device:TPU:1, one launch (start us, length us, event | category | flops | bytes accessed | tf_op | source)
XLA Modules:
  0.0 59.5 jit_solution(858744355361766839)
XLA Ops:
  0.7 0.0 copy-start.1
  0.7 0.0 copy-start
  0.7 0.0 copy-start.2
  0.7 0.6 %copy-done.1 = bf16[8,1,128]{2,0,1:T(8,128)(2,1)S(1)} copy-done((bf16[8,1,128]{2,0,1:T(8,128)(2,1)S(1)}, bf16[8,1,128]{2,0,1:T(8,128)(2,1)}, u32[]{:S(2)}) %copy-start.1) | copy-done | bytes 2072
  1.3 0.0 copy-done
  1.4 0.0 copy-done.2
  1.4 57.5 %whole_layer.1 = bf16[8,1024]{1,0:T(8,128)(2,1)S(1)} custom-call(bf16[8,1024]{1,0:T(8,128)(2,1)} %residual_hbm.1, bf16[8,1024]{1,0:T(8,128)(2,1)} %queries_hbm.1, bf16[8,512,128]{2,1,0:T(8,128)(2,1)} %bitcast.8, bf16[8,512,128]{2,1,0:T(8,128)(2,1)} %bitcast.9, bf16[8,128]{1,0:T(8,128)(2,1)S(1)} %bitcast.6, bf16[8,128]{1,0:T(8,128)(2,1)S(1)} %bitcast.7, ...), custom_call_target="tpu_custom_call" | custom-call | flops 1430000000 | bytes 5000000 | tf_op jit(solution)/shard_map/whole_layer/pallas_call | solution.py:445
  58.8 0.7 %broadcast_select_fusion = bf16[8,1024]{1,0:T(8,128)(2,1)} fusion(bf16[8,1024]{1,0:T(8,128)(2,1)S(1)} %whole_layer.1, pred[8]{0:T(512)(128)(4,1)S(1)} %iota_compare_fusion), kind=kLoop, calls=%fused_computation | loop fusion | flops 8192 | bytes 32776 | tf_op jit(solution)/shard_map/jit(_where)/select_n | solution.py:535
  (1 shorter events, 0.0 us)
Async XLA Ops:
  0.7 0.7 %copy-start.1 = (bf16[8,1,128]{2,0,1:T(8,128)(2,1)S(1)}, bf16[8,1,128]{2,0,1:T(8,128)(2,1)}, u32[]{:S(2)}) copy-start(bf16[8,1,128]{2,0,1:T(8,128)(2,1)} %param.17) | copy-start | bytes 6148
  0.7 0.7 %copy-start = (bf16[8,1,128]{2,0,1:T(8,128)(2,1)S(1)}, bf16[8,1,128]{2,0,1:T(8,128)(2,1)}, u32[]{:S(2)}) copy-start(bf16[8,1,128]{2,0,1:T(8,128)(2,1)} %param.16) | copy-start | bytes 6148
  0.7 0.7 %copy-start.2 = (s32[8]{0:T(128)S(1)}, s32[8]{0:T(128)}, u32[]{:S(2)}) copy-start(s32[8]{0:T(128)} %lengths_hbm.1) | copy-start | bytes 100
